TPU v7x, 32 devices: a whole 2x2x4 slice. The times are simulated.
32 devices in a mesh: grp: 4 (over y, x), dev: 8 (over z, core).
Axes of the slice: x: 2, y: 2, z: 4, core: 2. Of those that a mesh axis runs over, the one named last changes fastest.
Arguments:
- points: float32 [3, 32768], P(None, ('grp', 'dev')), may hold values from 0 to 2
- charges: float32 [16, 32768], P(None, ('grp', 'dev')), may hold values from -6 to 6
- morton: int32 [32768], P(('grp', 'dev')), may hold values from 0 to 1023, as said below
- neighbours: int32 [128, 8], P(('grp', 'dev')), may hold values from 0 to 127, as said below
- counts: int32 [128], P(('grp', 'dev')), may hold values from 1 to 8
- skel_leaf: float32 [3, 32768], P(None, ('grp', 'dev')), may hold values from 0 to 2
- skel_block: float32 [3, 8192], P(None, ('grp', 'dev')), may hold values from 0 to 2
- skel_group: float32 [3, 1024], replicated, may hold values from 0 to 2
Outputs:
- potential: float32 [16, 32768], P(None, ('grp', 'dev'))
Inputs may be any that keep to these rules, and one draw needn't show every extreme that they name: `morton`: each aligned run of 1024 entries is a permutation of 0 to 1023. `neighbours`: entry [q, k] is a leaf other than q, at most 4 leaves away from q; only slots k < counts[q] are used.
All inputs are finite; a program needn't handle non-finite values.
Results may differ from a plain program's by a relative error of at most 0.0003.
Values sent between devices are 32-bit elements; how exact they have to be, the bound alone decides.
A program may use at most 64 MiB of HBM per device.

v0:
```python
import math

import jax
import jax.numpy as jnp
from jax import lax
from jax.sharding import PartitionSpec as P

width_sq = 0.1
gain_factor = 5.0


def extended_2(cells, sides, width):
    for axis, dim in sides:
        count = lax.axis_size(axis)
        ends = count - 1
        head = lax.slice_in_dim(cells, 0, width, axis=dim)
        tail = lax.slice_in_dim(cells, cells.shape[dim] - width, cells.shape[dim], axis=dim)
        cells = jnp.concatenate(
            [
                lax.ppermute(tail, axis, [(i, (i + 1) % count) for i in range(ends)]),
                cells,
                lax.ppermute(head, axis, [((i + 1) % count, i) for i in range(ends)]),
            ],
            axis=dim,
        )
    return cells


def kernel_tile(source, target):
    distance = (source[0][:, None] - target[0][None, :]) ** 2
    distance = distance + (source[1][:, None] - target[1][None, :]) ** 2
    distance = distance + (source[2][:, None] - target[2][None, :]) ** 2
    return jnp.exp(-distance / width_sq)


def translate(values, source, target, term_count):
    product = jnp.dot(
        values,
        kernel_tile(source, target),
        precision=lax.Precision.HIGHEST,
        preferred_element_type=jnp.float32,
    )
    return gain_factor / math.sqrt(term_count) * product


def far_sum(running, weights, skeleton, target, own_member, skel_rank, term_count):
    span_cols = weights.shape[1]
    block_cols = min(skel_rank, span_cols)

    def one_block(block_index, partial_value):
        column = block_index * block_cols
        piece_w = lax.dynamic_slice_in_dim(weights, column, block_cols, 1)
        piece_s = lax.dynamic_slice_in_dim(skeleton, column, block_cols, 1)
        member = column // skel_rank
        keep_mask = jnp.where(member == own_member, 0.0, 1.0)
        return partial_value + keep_mask * translate(piece_w, piece_s, target, term_count)

    return lax.fori_loop(0, span_cols // block_cols, one_block, running)


def body(points, charges, morton, neighbours, counts, skel_leaf, skel_block, skel_group):
    n_groups = lax.axis_size("grp")
    n_blocks = lax.axis_size("dev")
    vectors, block_pts = charges.shape
    leaf_count = counts.shape[0]
    leaf_size = block_pts // leaf_count
    skel_rank = skel_block.shape[1]
    slot_total = neighbours.shape[1]
    group_id = lax.axis_index("grp")
    member_id = lax.axis_index("dev")
    block_id = group_id * n_blocks + member_id
    sorted_pts = jnp.take(points, morton, axis=1)
    sorted_chg = jnp.take(charges, morton, axis=1)
    leaf_pts = sorted_pts.reshape(3, leaf_count, leaf_size).transpose(1, 0, 2)
    leaf_chg = sorted_chg.reshape(vectors, leaf_count, leaf_size).transpose(1, 0, 2)
    leaf_skel = skel_leaf.reshape(3, leaf_count, skel_rank).transpose(1, 0, 2)
    leaf_weights = lax.map(
        lambda inputs: translate(inputs[0], inputs[1], inputs[2], leaf_size),
        (leaf_chg, leaf_pts, leaf_skel),
    )
    lifted = lax.map(
        lambda inputs: translate(inputs[0], inputs[1], skel_block, leaf_count * skel_rank),
        (leaf_weights, leaf_skel),
    )
    block_weights = jnp.sum(lifted, axis=0)
    own_group = lax.dynamic_slice_in_dim(skel_group, group_id * skel_rank, skel_rank, 1)
    raised = translate(block_weights, skel_block, own_group, n_blocks * skel_rank)
    empty = jnp.zeros((vectors, skel_rank), jnp.float32)
    group_terms = (n_groups - 1) * skel_rank
    group_weights = lax.psum(raised, "dev")
    group_field = far_sum(
        empty,
        lax.all_gather(group_weights, "grp", axis=1, tiled=True),
        skel_group,
        own_group,
        group_id,
        skel_rank,
        group_terms,
    )
    peer_field = far_sum(
        empty,
        lax.all_gather(block_weights, "dev", axis=1, tiled=True),
        lax.all_gather(skel_block, "dev", axis=1, tiled=True),
        skel_block,
        member_id,
        skel_rank,
        (n_blocks - 1) * skel_rank,
    )
    block_field = peer_field + translate(group_field, own_group, skel_block, skel_rank)
    leaf_field = lax.map(
        lambda target: translate(block_field, skel_block, target, skel_rank), leaf_skel
    )
    stacked = jnp.concatenate([sorted_pts, sorted_chg], axis=0)
    extended = extended_2(stacked, ((("grp", "dev"), 1),), block_pts)
    ext_leaves = extended.reshape(3 + vectors, 3 * leaf_count, leaf_size).transpose(1, 0, 2)
    first_leaf = block_id * leaf_count - leaf_count

    def near_leaf(inputs):
        own_pts, own_chg, own_field, own_skel, row_nbr, row_count = inputs
        direct = translate(own_chg, own_pts, own_pts, leaf_size)
        direct = direct + translate(own_field, own_skel, own_pts, skel_rank)

        def one_slot(slot_index, running):
            source = lax.dynamic_index_in_dim(
                ext_leaves, row_nbr[slot_index] - first_leaf, 0, keepdims=False
            )
            tile_term = translate(source[3:], source[:3], own_pts, leaf_size)
            return running + jnp.where(slot_index < row_count, tile_term, jnp.zeros_like(tile_term))

        return lax.fori_loop(0, slot_total, one_slot, direct)

    potential = lax.map(near_leaf, (leaf_pts, leaf_chg, leaf_field, leaf_skel, neighbours, counts))
    return potential.transpose(1, 0, 2).reshape(vectors, block_pts)


def solution(mesh):
    return jax.shard_map(
        body,
        mesh=mesh,
        in_specs=(
            P(None, ("grp", "dev")),
            P(None, ("grp", "dev")),
            P(("grp", "dev")),
            P(("grp", "dev"), None),
            P(("grp", "dev")),
            P(None, ("grp", "dev")),
            P(None, ("grp", "dev")),
            P(),
        ),
        out_specs=P(None, ("grp", "dev")),
        check_vma=False,
    )
```

profile of v0, /device:TPU:0, one launch (start us, length us, event | category | flops | bytes accessed | tf_op | source)
XLA Modules:
  0.0 182.4 jit_solution(1003156608991850524)
XLA Ops:
  0.0 0.8 compare_and_fusion
  0.8 0.9 copy.25
  1.7 2.8 %gather_fusion.1 = f32[1024,3]{1,0:T(8,128)S(1)} fusion(f32[3,1024]{0,1:T(8,128)S(1)} %copy.25, s32[1024]{0:T(1024)S(1)} %fusion.219), kind=kCustom, calls=%fused_computation.1 | custom fusion | bytes 28672 | tf_op jit(solution)/shard_map/jit(_take)/gather | solution.py:72
  5.8 2.8 %gather_fusion = f32[1024,16]{1,0:T(8,128)S(1)} fusion(f32[16,1024]{0,1:T(8,128)S(1)} %copy.23, s32[1024]{0:T(1024)S(1)} %fusion.219), kind=kCustom, calls=%fused_computation | custom fusion | bytes 135168 | tf_op jit(solution)/shard_map/jit(_take)/gather | solution.py:73
  9.0 1.3 collective-permute-start.1
  10.3 3.0 %collective-permute-start = (f32[19,1024]{1,0:T(8,128)S(1)}, f32[19,1024]{1,0:T(8,128)S(1)}, u32[]{:S(2)}, u32[]{:S(2)}) collective-permute-start(f32[19,1024]{1,0:T(8,128)S(1)} %pad_maximum_fusion.1), channel_id=1, source_target_pairs={{0,1},{1,2},{2,3},{3,4},{4,5},{5,6},{6,7},{7,8},{8,9},{9,10},{10,1... | collective-permute-start | bytes 233480 | tf_op jit(solution)/shard_map/ppermute | solution.py:20
  14.1 19.0 %all_gather.10 = f32[3,2048]{1,0:T(4,128)S(1)} all-gather(f32[3,256]{1,0:T(4,128)S(1)} %copy-done), channel_id=1, replica_groups=mesh['grp'=4,'dev'=8] {'dev'}, dimensions={1}, use_global_device_ids=true | all-gather | bytes 27648 | tf_op jit(solution)/shard_map/all_gather | solution.py:103
  33.5 0.7 copy-done.1
  34.2 1.6 while.85
  35.8 1.7 while.86
  37.6 14.0 %all_gather.9 = f32[16,2048]{1,0:T(8,128)S(1)} all-gather(f32[16,256]{1,0:T(8,128)S(1)} %reduce_sum.9), channel_id=1, replica_groups=mesh['grp'=4,'dev'=8] {'dev'}, dimensions={1}, use_global_device_ids=true | all-gather | bytes 147456 | tf_op jit(solution)/shard_map/all_gather | solution.py:102
  52.0 26.5 %psum.7 = f32[16,256]{1,0:T(8,128)S(1)} all-reduce(f32[16,256]{1,0:T(8,128)S(1)} %convolution_multiply_fusion.7), channel_id=1, replica_groups=mesh['grp'=4,'dev'=8] {'dev'}, use_global_device_ids=true, to_apply=%region_7.8 | all-reduce | flops 4096 | bytes 32768 | tf_op jit(solution)/shard_map/psum | solution.py:90
  78.5 9.1 %all_gather.11 = f32[16,1024]{1,0:T(8,128)S(1)} all-gather(f32[16,256]{1,0:T(8,128)S(1)} %psum.7), channel_id=1, replica_groups=mesh['grp'=4,'dev'=8] {'grp'}, dimensions={1}, use_global_device_ids=true | all-gather | bytes 81920 | tf_op jit(solution)/shard_map/all_gather | solution.py:93
  87.6 2.1 %while.91 = (s32[]{:T(128)}, f32[16,256]{1,0:T(8,128)S(1)}, f32[16,1024]{1,0:T(8,128)S(1)}, f32[3,1024]{1,0:T(4,128)S(1)}, f32[3,256]{1,0:T(4,128)S(1)}, /*index...) while((s32[]{:T(128)}, f32[16,256]{1,0:T(8,128)S(1)}, ...), condition=%wide.region_9.10_spmd.clone, body=%wide.region_8.9_spmd.clone.sunk | while | flops 13250586 | bytes 68032 | solution.py:58
  89.7 4.3 %while.90 = (s32[]{:T(128)}, f32[16,256]{1,0:T(8,128)S(1)}, f32[16,2048]{1,0:T(8,128)S(1)}, f32[3,2048]{1,0:T(4,128)S(1)}, f32[3,256]{1,0:T(4,128)S(1)}, /*index...) while((s32[]{:T(128)}, f32[16,256]{1,0:T(8,128)S(1)}, ...), condition=%wide.region_6.7_spmd.clone, body=%wide.region_5.6_spmd.clone.sunk | while | flops 13250586 | bytes 68032 | solution.py:58
  94.4 1.8 while.87
  97.1 84.6 %while.89 = (s32[]{:T(128)}, f32[4,16,256]{2,1,0:T(8,128)S(1)}, f32[4,16,256]{2,1,0:T(8,128)S(1)}, f32[4,3,256]{2,1,0:T(4,128)S(1)}, f32[4,16,256]{2,1,0:T(8,128...) while((s32[]{:T(128)}, f32[4,16,256]{2,1,0:T(8,128)S(1)}, ...), condition=%wide.region_15.16_spmd, body=%wide.region_12.15_spmd.sunk | while | flops 39735312 | bytes 213682 | solution.py:132
  97.8 0.7 fusion.275
  99.3 19.0 %while.92 = (s32[]{:T(128)}, f32[16,256]{1,0:T(8,128)S(1)}, s32[]{:T(128)}, s32[8]{0:T(128)S(1)}, s32[]{:T(128)}, /*index=5*/f32[12,19,256]{2,1,0:T(8,128)S(1)},...) while((s32[]{:T(128)}, f32[16,256]{1,0:T(8,128)S(1)}, ...), condition=%wide.region_14.14_spmd, body=%wide.region_13.13_spmd.sunk | while | flops 13250570 | bytes 67841 | solution.py:130
  99.9 0.7 dynamic_slice.147
  102.3 0.7 dynamic_slice.147
  104.6 0.7 dynamic_slice.147
  107.0 0.7 dynamic_slice.147
  109.4 0.7 dynamic_slice.147
  111.8 0.7 dynamic_slice.147
  114.1 0.7 dynamic_slice.147
  116.5 0.7 dynamic_slice.147
  118.9 0.7 fusion.275
  120.4 19.0 %while.92 = (s32[]{:T(128)}, f32[16,256]{1,0:T(8,128)S(1)}, s32[]{:T(128)}, s32[8]{0:T(128)S(1)}, s32[]{:T(128)}, /*index=5*/f32[12,19,256]{2,1,0:T(8,128)S(1)},...) while((s32[]{:T(128)}, f32[16,256]{1,0:T(8,128)S(1)}, ...), condition=%wide.region_14.14_spmd, body=%wide.region_13.13_spmd.sunk | while | flops 13250570 | bytes 67841 | solution.py:130
  121.0 0.7 dynamic_slice.147
  130.5 0.7 dynamic_slice.147
  132.9 0.7 dynamic_slice.147
  135.3 0.7 dynamic_slice.147
  137.7 0.7 dynamic_slice.147
  140.1 0.7 fusion.275
  141.6 19.0 %while.92 = (s32[]{:T(128)}, f32[16,256]{1,0:T(8,128)S(1)}, s32[]{:T(128)}, s32[8]{0:T(128)S(1)}, s32[]{:T(128)}, /*index=5*/f32[12,19,256]{2,1,0:T(8,128)S(1)},...) while((s32[]{:T(128)}, f32[16,256]{1,0:T(8,128)S(1)}, ...), condition=%wide.region_14.14_spmd, body=%wide.region_13.13_spmd.sunk | while | flops 13250570 | bytes 67841 | solution.py:130
  142.2 0.7 dynamic_slice.147
  151.7 0.7 dynamic_slice.147
  154.1 0.7 dynamic_slice.147
  156.4 0.7 dynamic_slice.147
  158.8 0.7 dynamic_slice.147
  161.2 0.7 fusion.275
  162.7 19.0 %while.92 = (s32[]{:T(128)}, f32[16,256]{1,0:T(8,128)S(1)}, s32[]{:T(128)}, s32[8]{0:T(128)S(1)}, s32[]{:T(128)}, /*index=5*/f32[12,19,256]{2,1,0:T(8,128)S(1)},...) while((s32[]{:T(128)}, f32[16,256]{1,0:T(8,128)S(1)}, ...), condition=%wide.region_14.14_spmd, body=%wide.region_13.13_spmd.sunk | while | flops 13250570 | bytes 67841 | solution.py:130
  163.3 0.7 dynamic_slice.147
  172.8 0.7 dynamic_slice.147
  175.2 0.7 dynamic_slice.147
  177.6 0.7 dynamic_slice.147
  180.0 0.7 dynamic_slice.147
  (226 shorter events, 40.5 us)
Async XLA Ops:
  0.0 0.8 copy-start.4
  4.7 0.8 copy-start.2
  9.0 87.2 %collective-permute-start.1 = (f32[19,1024]{1,0:T(8,128)S(1)}, f32[19,1024]{1,0:T(8,128)S(1)}, u32[]{:S(2)}, u32[]{:S(2)}) collective-permute-start(f32[19,1024]{1,0:T(8,128)S(1)} %pad_maximum_fusion.1), channel_id=1, source_target_pairs={{1,0},{2,1},{3,2},{4,3},{5,4},{6,5},{7,6},{8,7},{9,8},{10,9},{11,1... | collective-permute-start | bytes 233480 | tf_op jit(solution)/shard_map/ppermute | solution.py:22
  10.3 85.9 %collective-permute-start = (f32[19,1024]{1,0:T(8,128)S(1)}, f32[19,1024]{1,0:T(8,128)S(1)}, u32[]{:S(2)}, u32[]{:S(2)}) collective-permute-start(f32[19,1024]{1,0:T(8,128)S(1)} %pad_maximum_fusion.1), channel_id=1, source_target_pairs={{0,1},{1,2},{2,3},{3,4},{4,5},{5,6},{6,7},{7,8},{8,9},{9,10},{10,1... | collective-permute-start | bytes 233480 | tf_op jit(solution)/shard_map/ppermute | solution.py:20
  13.4 0.7 copy-start
  33.4 0.7 copy-start.1
  37.6 14.0 %copy-start.3 = (f32[3,1024]{1,0:T(4,128)S(1)}, f32[3,1024]{1,0:T(4,128)}, u32[]{:S(2)}) copy-start(f32[3,1024]{1,0:T(4,128)} %param.29) | copy-start | bytes 36868
  96.5 0.7 copy-start.5
where the time goes:
time: 183 us; the launch traced here: 182 us
  blocking collectives  68.5 us (37%)
  loops' own time  42.9 us (23%)
  local copies, waits for them, and re-layouts  39.2 us (21%)
  matrix products  25.8 us (14%)
  starting transfers between devices  4.33 us (2%)
    another operation x4, loops' own time, near_leaf(): return lax.fori_loop(0, slot_total, one_slot, direct)  41.6 us
    psum x1, blocking collectives, body(): group_weights = lax.psum(raised, 'dev')  26.5 us
    dot_general x66, matrix products, translate(): jnp.dot(values, kernel_tile(source, target), precision=lax.Precision.HIGH...  25.8 us
    dynamic_slice x32, local copies, waits for them, and re-layouts, one_slot(): row_nbr[slot_index] - first_leaf  20.9 us
    all_gather x1, blocking collectives, body(): lax.all_gather(skel_block, 'dev', axis=1, tiled=True)  19 us
    all_gather x1, blocking collectives, body(): lax.all_gather(block_weights, 'dev', axis=1, tiled=True)  14 us
    all_gather x1, blocking collectives, body(): lax.all_gather(group_weights, 'grp', axis=1, tiled=True)  9.11 us
    unnamed x14, local copies, waits for them, and re-layouts  3.77 us
  transfers between devices with their start and end apart: 2, of which 0 were waited for; matrix products, arithmetic and copies ran while one was open for 6% of the time, Pallas kernels for 0%

commit v1 on v0

v1 whole, which is shorter than its diff:
```python
import functools
import math

import jax
import jax.numpy as jnp
from jax import lax
from jax.experimental import pallas as pl
from jax.experimental.pallas import tpu as pltpu
from jax.sharding import PartitionSpec as P

width_sq = 0.1
gain_factor = 5.0
to_base_two = math.sqrt(math.log2(math.e) / width_sq)
middle = 1.0
FEAT = 64
ROWS = 8
MESH = pl.DeviceIdType.MESH
f32, bf16 = jnp.float32, jnp.bfloat16


def parts(x, count):
    out = []
    for _ in range(count - 1):
        out.append(x.astype(bf16).astype(f32))
        x = x - out[-1]
    out.append(x.astype(bf16).astype(f32))
    return out


def features(coords):
    row = lax.broadcasted_iota(jnp.int32, coords.shape, 0)
    c = jnp.where(row < 3, (coords - middle) * to_base_two, 0.0)
    norm = jnp.broadcast_to(jnp.sum(c * c, axis=0, keepdims=True), c.shape)
    hi, mid, lo = parts(c, 3)
    n0, n1, n2 = parts(norm, 3)
    one = jnp.ones_like(c)
    zero = jnp.zeros_like(c)
    first = jnp.where(row == 0, n0, jnp.where(row == 1, n1, n2))
    second = jnp.where(row == 3, n0, jnp.where(row == 4, n1, n2))
    src_n = jnp.where(row < 3, first, jnp.where(row < 6, one, zero))
    tgt_n = jnp.where(row < 3, -one, jnp.where(row < 6, -second, zero))
    hi2, mid2, lo2 = hi + hi, mid + mid, lo + lo
    src = jnp.concatenate([hi, hi, mid, mid, hi, lo, src_n, zero], axis=0)
    tgt = jnp.concatenate([hi2, mid2, hi2, mid2, lo2, hi2, tgt_n, zero], axis=0)
    return src, tgt


def split_rows(v):
    return jnp.concatenate(parts(v, 2), axis=0).astype(bf16)


def apply_kernel(v2, src, tgt):
    half = v2.shape[0] // 2
    k = jnp.exp2(jnp.dot(src, tgt, preferred_element_type=f32))
    k_hi = k.astype(bf16)
    k_lo = (k - k_hi.astype(f32)).astype(bf16)
    r = jnp.dot(v2, k_hi, preferred_element_type=f32)
    return r[:half] + r[half:] + jnp.dot(v2[:half], k_lo, preferred_element_type=f32)


def kernel(
    n_groups, n_blocks, leaf_count, leaf_size, rank, slots,
    points, charges, morton, neighbours, counts, skel_leaf, skel_block, skel_group,
    out,
    pad, halo_out, halo_left, halo_right, skel_all, bw_all, gw_all,
    ext_src, ext_v, own_tgt, leaf_src, leaf_tgt, grp_src, blk_src, two_tgt,
    halo_send, halo_recv, skel_send, skel_recv, bw_send, bw_recv, gw_send, gw_recv,
):
    vectors = charges.shape[0]
    block_pts = leaf_count * leaf_size
    g = lax.axis_index("grp")
    m = lax.axis_index("dev")
    block = g * n_blocks + m
    total = n_groups * n_blocks
    right = lax.rem(block + 1, total)
    left = lax.rem(block + total - 1, total)
    right_id = (right // n_blocks, lax.rem(right, n_blocks))
    left_id = (left // n_blocks, lax.rem(left, n_blocks))
    peers = [(g, lax.rem(m + d, n_blocks)) for d in range(1, n_blocks)]
    cousins = [(lax.rem(g + d, n_groups), m) for d in range(1, n_groups)]

    barrier = pltpu.get_barrier_semaphore()
    greeted = [left_id, right_id] + peers + cousins
    for who in greeted:
        pl.semaphore_signal(barrier, inc=1, device_id=who, device_id_type=MESH)

    def scale(terms):
        return gain_factor / math.sqrt(terms)

    pad[...] = jnp.zeros_like(pad)
    pad[0:3, 0:block_pts] = points[...]
    pts = pad[:, 0:block_pts]
    pad[0:3, 0:rank] = skel_block[...]
    skel_all[pl.ds(m, 1)] = pad[:, 0:rank][None]

    stacked = jnp.concatenate(
        parts(pts, 3) + [jnp.zeros_like(pts)] + parts(charges[...], 2), axis=0
    ).astype(bf16)
    place = lax.broadcasted_iota(jnp.int32, (block_pts, leaf_size), 0)
    for i in range(leaf_count):
        cols = slice(i * leaf_size, (i + 1) * leaf_size)
        onehot = jnp.where(place == morton[0:1, cols], 1.0, 0.0).astype(bf16)
        s = jnp.dot(stacked, onehot, preferred_element_type=f32)
        own = s[0:8] + s[8:16] + s[16:24]
        halo_out[0:ROWS, cols] = own
        halo_out[ROWS:, cols] = s[32 : 32 + vectors] + s[32 + vectors :]
        ext_v[leaf_count + i] = s[32:].astype(bf16)

    pl.semaphore_wait(barrier, len(greeted))

    def to_peer(buf, send, recv, k, who, slot):
        return pltpu.make_async_remote_copy(
            src_ref=buf.at[slot], dst_ref=buf.at[slot],
            send_sem=send.at[k], recv_sem=recv.at[slot],
            device_id=who, device_id_type=MESH,
        )

    skel_copies = [to_peer(skel_all, skel_send, skel_recv, k, who, m) for k, who in enumerate(peers)]
    for c in skel_copies:
        c.start()
    halo_copies = [
        pltpu.make_async_remote_copy(
            src_ref=halo_out, dst_ref=dst, send_sem=halo_send.at[k], recv_sem=halo_recv.at[k],
            device_id=who, device_id_type=MESH,
        )
        for k, (dst, who) in enumerate([(halo_left, right_id), (halo_right, left_id)])
    ]
    for c in halo_copies:
        c.start()

    src, tgt = features(halo_out[0:ROWS])
    ext_src[block_pts : 2 * block_pts] = src.T.astype(bf16)
    own_tgt[...] = tgt.astype(bf16)
    pad[0:3, 0 : leaf_count * rank] = skel_leaf[...]
    src, tgt = features(pad[:, 0 : leaf_count * rank])
    leaf_src[...] = src.T.astype(bf16)
    leaf_tgt[...] = tgt.astype(bf16)
    _, tgt = features(skel_all[pl.ds(m, 1)][0])
    two_tgt[:, rank:] = tgt.astype(bf16)

    bw = jnp.zeros((vectors, rank), f32)
    for i in range(leaf_count):
        pc = slice(block_pts + i * leaf_size, block_pts + (i + 1) * leaf_size)
        kc = slice(i * rank, (i + 1) * rank)
        lw = apply_kernel(ext_v[leaf_count + i], ext_src[pc], leaf_tgt[:, kc]) * scale(leaf_size)
        bw = bw + apply_kernel(split_rows(lw), leaf_src[kc], two_tgt[:, rank:])
    bw_all[pl.ds(m, 1)] = (bw * scale(leaf_count * rank))[None]
    bw_copies = [to_peer(bw_all, bw_send, bw_recv, k, who, m) for k, who in enumerate(peers)]
    for c in bw_copies:
        c.start()

    for j in range(n_groups):
        pad[0:3, 0:rank] = skel_group[:, j * rank : (j + 1) * rank]
        src, tgt = features(pad[:, 0:rank])
        grp_src[j * rank : (j + 1) * rank] = src.T.astype(bf16)
        pl.when(g == j)(functools.partial(two_tgt.__setitem__, (slice(None), slice(0, rank)), tgt.astype(bf16)))

    for c, buf, base in zip(halo_copies, (halo_left, halo_right), (0, 2 * leaf_count)):
        c.wait_recv()
        src, _ = features(buf[0:ROWS])
        ext_src[base * leaf_size : base * leaf_size + block_pts] = src.T.astype(bf16)
        for i in range(leaf_count):
            ext_v[base + i] = split_rows(buf[ROWS:, i * leaf_size : (i + 1) * leaf_size])

    first_leaf = block * leaf_count - leaf_count
    window = 2 * leaf_count + 1

    def near(i, carry):
        tcol = pl.ds(pl.multiple_of(i * leaf_size, leaf_size), leaf_size)
        target = own_tgt[:, tcol]
        acc = jnp.zeros((vectors, leaf_size), f32)
        for o in range(window):
            e = i + o
            srow = pl.ds(pl.multiple_of(e * leaf_size, leaf_size), leaf_size)
            term = apply_kernel(ext_v[e], ext_src[srow], target)
            if o == leaf_count:
                acc = acc + term
            else:
                times = jnp.int32(0)
                for k in range(slots):
                    hit = (neighbours[i, k] - first_leaf == e) & (k < counts[i])
                    times = times + jnp.where(hit, 1, 0)
                acc = acc + times.astype(f32) * term
        out[:, tcol] = acc * scale(leaf_size)
        return carry

    lax.fori_loop(0, leaf_count // 2, near, 0)

    for j, c in enumerate(peers):
        k = c[1]
        to_peer(skel_all, skel_send, skel_recv, j, c, k).wait_recv()
        to_peer(bw_all, bw_send, bw_recv, j, c, k).wait_recv()

    def from_block(b, carry):
        gw, field = carry
        src, _ = features(skel_all[b])
        r = apply_kernel(split_rows(bw_all[b]), src.T.astype(bf16), two_tgt[...])
        keep = jnp.where(b == m, 0.0, 1.0)
        return gw + r[:, :rank], field + keep * r[:, rank:]

    empty = jnp.zeros((vectors, rank), f32)
    gw, field = lax.fori_loop(0, n_blocks, from_block, (empty, empty))
    field = field * scale((n_blocks - 1) * rank)
    gw_all[pl.ds(g, 1)] = (gw * scale(n_blocks * rank))[None]
    gw_copies = [to_peer(gw_all, gw_send, gw_recv, k, who, g) for k, who in enumerate(cousins)]
    for c in gw_copies:
        c.start()

    lax.fori_loop(leaf_count // 2, leaf_count, near, 0)

    for j, c in enumerate(cousins):
        to_peer(gw_all, gw_send, gw_recv, j, c, c[0]).wait_recv()

    def from_group(h, acc):
        srow = pl.ds(pl.multiple_of(h * rank, rank), rank)
        keep = jnp.where(h == g, 0.0, 1.0)
        return acc + keep * apply_kernel(split_rows(gw_all[h]), grp_src[srow], two_tgt[:, :rank])

    gfield = lax.fori_loop(0, n_groups, from_group, empty) * scale((n_groups - 1) * rank)
    own_rows = pl.ds(pl.multiple_of(g * rank, rank), rank)
    field = field + scale(rank) * apply_kernel(split_rows(gfield), grp_src[own_rows], two_tgt[:, rank:])
    src, _ = features(skel_all[pl.ds(m, 1)][0])
    blk_src[...] = src.T.astype(bf16)
    field2 = split_rows(field)
    for i in range(leaf_count):
        kc = slice(i * rank, (i + 1) * rank)
        pc = slice(i * leaf_size, (i + 1) * leaf_size)
        lf = apply_kernel(field2, blk_src[...], leaf_tgt[:, kc]) * scale(rank)
        out[:, pc] += apply_kernel(split_rows(lf), leaf_src[kc], own_tgt[:, pc]) * scale(rank)

    for c in skel_copies + halo_copies + bw_copies + gw_copies:
        c.wait_send()


def body(n_groups, n_blocks, points, charges, morton, neighbours, counts, skel_leaf, skel_block, skel_group):
    vectors, block_pts = charges.shape
    leaf_count = counts.shape[0]
    leaf_size = block_pts // leaf_count
    rank = skel_block.shape[1]
    slots = neighbours.shape[1]
    vmem = pl.BlockSpec(memory_space=pltpu.VMEM)
    smem = pl.BlockSpec(memory_space=pltpu.SMEM)
    wide = max(block_pts, leaf_count * rank)
    dma = pltpu.SemaphoreType.DMA
    return pl.pallas_call(
        functools.partial(kernel, n_groups, n_blocks, leaf_count, leaf_size, rank, slots),
        out_shape=jax.ShapeDtypeStruct((vectors, block_pts), f32),
        in_specs=[vmem, vmem, vmem, smem, smem, vmem, vmem, vmem],
        out_specs=vmem,
        scratch_shapes=[
            pltpu.VMEM((ROWS, wide), f32),
            pltpu.VMEM((ROWS + vectors, block_pts), f32),
            pltpu.VMEM((ROWS + vectors, block_pts), f32),
            pltpu.VMEM((ROWS + vectors, block_pts), f32),
            pltpu.VMEM((n_blocks, ROWS, rank), f32),
            pltpu.VMEM((n_blocks, vectors, rank), f32),
            pltpu.VMEM((n_groups, vectors, rank), f32),
            pltpu.VMEM((3 * block_pts, FEAT), bf16),
            pltpu.VMEM((3 * leaf_count, 2 * vectors, leaf_size), bf16),
            pltpu.VMEM((FEAT, block_pts), bf16),
            pltpu.VMEM((leaf_count * rank, FEAT), bf16),
            pltpu.VMEM((FEAT, leaf_count * rank), bf16),
            pltpu.VMEM((n_groups * rank, FEAT), bf16),
            pltpu.VMEM((rank, FEAT), bf16),
            pltpu.VMEM((FEAT, 2 * rank), bf16),
            dma((2,)),
            dma((2,)),
            dma((n_blocks - 1,)),
            dma((n_blocks,)),
            dma((n_blocks - 1,)),
            dma((n_blocks,)),
            dma((n_groups - 1,)),
            dma((n_groups,)),
        ],
        compiler_params=pltpu.CompilerParams(
            collective_id=0, has_side_effects=True, vmem_limit_bytes=40 * 1024 * 1024
        ),
    )(points, charges, morton.reshape(1, block_pts), neighbours, counts, skel_leaf, skel_block, skel_group)


def solution(mesh):
    return jax.shard_map(
        functools.partial(body, mesh.shape["grp"], mesh.shape["dev"]),
        mesh=mesh,
        in_specs=(
            P(None, ("grp", "dev")),
            P(None, ("grp", "dev")),
            P(("grp", "dev")),
            P(("grp", "dev"), None),
            P(("grp", "dev")),
            P(None, ("grp", "dev")),
            P(None, ("grp", "dev")),
            P(),
        ),
        out_specs=P(None, ("grp", "dev")),
        check_vma=False,
    )
```

time: 183 us -> 30.8 us (0.17)
  blocking collectives: 68.5 us -> 0 us
  loops' own time: 42.9 us -> 0 us
  local copies, waits for them, and re-layouts: 39.2 us -> 6.33 us
  matrix products: 25.8 us -> 0 us
  Pallas kernels: 0 us -> 24 us
  starting transfers between devices: 4.33 us -> 0 us
    another operation x10 -> x0, loops' own time: 42.9 us -> none  [the longest x4 41.6 us: near_leaf(): return lax.fori_loop(0, slot_total, one_slot, direct)]
    all_gather x3 -> x0, blocking collectives: 42.1 us -> none  [the longest x1 19 us: body(): lax.all_gather(skel_block, 'dev', axis=1, tiled=True)]
    psum x1 -> x0, blocking collectives: 26.5 us -> none  [body(): group_weights = lax.psum(raised, 'dev')]
    dot_general x66 -> x0, matrix products: 25.8 us -> none  [translate(): jnp.dot(values, kernel_tile(source, target), precision=lax.Precision.HIGH...]
    pallas_call x0 -> x1, Pallas kernels: none -> 24 us  [body(): pl.pallas_call(functools.partial(kernel, n_groups, n_blocks, leaf_count,...]
    dynamic_slice x37 -> x0, local copies, waits for them, and re-layouts: 23.4 us -> none  [the longest x32 20.9 us: one_slot(): row_nbr[slot_index] - first_leaf]
    gather x4 -> x0, local copies, waits for them, and re-layouts: 5.98 us -> none  [the longest x2 3 us: body(): sorted_pts = jnp.take(points, morton, axis=1)]
    ppermute x2 -> x0, starting transfers between devices: 4.33 us -> none  [the longest x1 3.04 us: extended_2(): lax.ppermute(tail, axis, [(i, (i + 1) % count) for i in range(ends)])]
  transfers between devices with their start and end apart: 2 -> 0, of which waited for: 0 -> 0; matrix products, arithmetic and copies ran while one was open for 6% -> 0% of each run, Pallas kernels for 0% -> 0%
where the time goes in v1:
time: 30.8 us; the launch traced here: 30.3 us
  Pallas kernels  24 us (78%)
  local copies, waits for them, and re-layouts  6.33 us (21%)
    pallas_call x1, Pallas kernels, body(): pl.pallas_call(functools.partial(kernel, n_groups, n_blocks, leaf_count,...  24 us
    unnamed x17, local copies, waits for them, and re-layouts  6.33 us

profile of v1, /device:TPU:0, one launch (start us, length us, event | category | flops | bytes accessed | tf_op | source)
XLA Modules:
  0.0 30.3 jit_solution(14066304700790222712)
XLA Ops:
  0.0 0.0 copy-start.7
  0.0 0.7 %copy-done.7 = s32[4]{0:T(128)S(1)} copy-done((s32[4]{0:T(128)S(1)}, s32[4]{0:T(128)}, u32[]{:S(2)}) %copy-start.7) | copy-done | bytes 40
  0.7 0.0 copy-start
  0.7 0.8 %copy-done = f32[16,1024]{1,0:T(8,128)S(1)} copy-done((f32[16,1024]{1,0:T(8,128)S(1)}, f32[16,1024]{1,0:T(8,128)}, u32[]{:S(2)}) %copy-start) | copy-done | bytes 65560
  1.5 0.0 copy-start.1
  1.5 0.7 %copy-done.1 = f32[3,1024]{1,0:T(4,128)S(1)} copy-done((f32[3,1024]{1,0:T(4,128)S(1)}, f32[3,1024]{1,0:T(4,128)}, u32[]{:S(2)}) %copy-start.1) | copy-done | bytes 12312
  2.2 0.0 copy-start.2
  2.2 0.7 %copy-done.2 = f32[3,1024]{1,0:T(4,128)S(1)} copy-done((f32[3,1024]{1,0:T(4,128)S(1)}, f32[3,1024]{1,0:T(4,128)}, u32[]{:S(2)}) %copy-start.2) | copy-done | bytes 12312
  2.9 0.0 copy-start.3
  2.9 0.7 %copy-done.3 = f32[3,1024]{1,0:T(4,128)S(1)} copy-done((f32[3,1024]{1,0:T(4,128)S(1)}, f32[3,1024]{1,0:T(4,128)}, u32[]{:S(2)}) %copy-start.3) | copy-done | bytes 12312
  3.6 0.0 copy-start.4
  3.7 0.7 %copy-done.4 = s32[1024]{0:T(1024)S(1)} copy-done((s32[1024]{0:T(1024)S(1)}, s32[1024]{0:T(1024)}, u32[]{:S(2)}) %copy-start.4) | copy-done | bytes 4120
  4.3 0.0 copy-start.5
  4.3 0.7 %copy-done.5 = f32[3,256]{1,0:T(4,128)S(1)} copy-done((f32[3,256]{1,0:T(4,128)S(1)}, f32[3,256]{1,0:T(4,128)}, u32[]{:S(2)}) %copy-start.5) | copy-done | bytes 3096
  5.0 0.0 copy-start.6
  5.0 0.7 %copy-done.6 = s32[4,8]{1,0:T(4,128)S(1)} copy-done((s32[4,8]{1,0:T(4,128)S(1)}, s32[4,8]{1,0:T(4,128)}, u32[]{:S(2)}) %copy-start.6) | copy-done | bytes 152
  5.7 24.0 %shard_map.82 = f32[16,1024]{1,0:T(8,128)S(1)} custom-call(f32[3,1024]{1,0:T(4,128)S(1)} %copy-done.1, f32[16,1024]{1,0:T(8,128)S(1)} %copy-done, s32[1,1024]{1,0:T(1,128)S(1)} %bitcast.1, s32[4,8]{1,0:T(4,128)S(1)} %copy-done.6, s32[4]{0:T(128)S(1)} %copy-done.7, f32[3,1024]{1,0:T(4,128)S(1)} %copy-done.2, f32[3,256]{1,0:T(4,128)S(1)} %copy-done.5, ...), custom_call_target="tpu_custom_call" | custom-call | tf_op jit(solution)/shard_map/pallas_call | solution.py:245
  29.7 0.6 %copy.10 = f32[16,1024]{1,0:T(8,128)} copy(f32[16,1024]{1,0:T(8,128)S(1)} %shard_map.82) | data formatting | bytes 131072
Async XLA Ops:
  0.0 0.7 %copy-start.7 = (s32[4]{0:T(128)S(1)}, s32[4]{0:T(128)}, u32[]{:S(2)}) copy-start(s32[4]{0:T(128)} %counts.1) | copy-start | bytes 52
  0.7 0.8 %copy-start = (f32[16,1024]{1,0:T(8,128)S(1)}, f32[16,1024]{1,0:T(8,128)}, u32[]{:S(2)}) copy-start(f32[16,1024]{1,0:T(8,128)} %charges.1) | copy-start | bytes 196612
  1.5 0.7 %copy-start.1 = (f32[3,1024]{1,0:T(4,128)S(1)}, f32[3,1024]{1,0:T(4,128)}, u32[]{:S(2)}) copy-start(f32[3,1024]{1,0:T(4,128)} %points.1) | copy-start | bytes 36868
  2.2 0.7 %copy-start.2 = (f32[3,1024]{1,0:T(4,128)S(1)}, f32[3,1024]{1,0:T(4,128)}, u32[]{:S(2)}) copy-start(f32[3,1024]{1,0:T(4,128)} %skel_leaf.1) | copy-start | bytes 36868
  2.9 0.7 %copy-start.3 = (f32[3,1024]{1,0:T(4,128)S(1)}, f32[3,1024]{1,0:T(4,128)}, u32[]{:S(2)}) copy-start(f32[3,1024]{1,0:T(4,128)} %skel_group.1) | copy-start | bytes 36868
  3.6 0.7 %copy-start.4 = (s32[1024]{0:T(1024)S(1)}, s32[1024]{0:T(1024)}, u32[]{:S(2)}) copy-start(s32[1024]{0:T(1024)} %param.10) | copy-start | bytes 12292
  4.3 0.7 %copy-start.5 = (f32[3,256]{1,0:T(4,128)S(1)}, f32[3,256]{1,0:T(4,128)}, u32[]{:S(2)}) copy-start(f32[3,256]{1,0:T(4,128)} %skel_block.1) | copy-start | bytes 9220
  5.0 0.7 %copy-start.6 = (s32[4,8]{1,0:T(4,128)S(1)}, s32[4,8]{1,0:T(4,128)}, u32[]{:S(2)}) copy-start(s32[4,8]{1,0:T(4,128)} %neighbours.1) | copy-start | bytes 388

commit v2 on v1

v2 whole, which is shorter than its diff:
```python
import functools
import math

import jax
import jax.numpy as jnp
from jax import lax
from jax.experimental import pallas as pl
from jax.experimental.pallas import tpu as pltpu
from jax.sharding import PartitionSpec as P

width_sq = 0.1
gain_factor = 5.0
to_base_two = math.sqrt(math.log2(math.e) / width_sq)
middle = 1.0
FEAT = 64
ROWS = 8
MESH = pl.DeviceIdType.MESH
f32, bf16 = jnp.float32, jnp.bfloat16


def parts(x, count):
    out = []
    for _ in range(count - 1):
        out.append(x.astype(bf16).astype(f32))
        x = x - out[-1]
    out.append(x.astype(bf16).astype(f32))
    return out


def features(coords):
    row = lax.broadcasted_iota(jnp.int32, coords.shape, 0)
    c = jnp.where(row < 3, (coords - middle) * to_base_two, 0.0)
    norm = jnp.broadcast_to(jnp.sum(c * c, axis=0, keepdims=True), c.shape)
    hi, mid, lo = parts(c, 3)
    n0, n1, n2 = parts(norm, 3)
    one = jnp.ones_like(c)
    zero = jnp.zeros_like(c)
    first = jnp.where(row == 0, n0, jnp.where(row == 1, n1, n2))
    second = jnp.where(row == 3, n0, jnp.where(row == 4, n1, n2))
    src_n = jnp.where(row < 3, first, jnp.where(row < 6, one, zero))
    tgt_n = jnp.where(row < 3, -one, jnp.where(row < 6, -second, zero))
    hi2, mid2, lo2 = hi + hi, mid + mid, lo + lo
    src = jnp.concatenate([hi, hi, mid, mid, hi, lo, src_n, zero], axis=0)
    tgt = jnp.concatenate([hi2, mid2, hi2, mid2, lo2, hi2, tgt_n, zero], axis=0)
    return src, tgt


def split_rows(v):
    return jnp.concatenate(parts(v, 2), axis=0).astype(bf16)


CHUNK = 64


def fill_kernel(src, tgt, k_hi, k_lo, row, col):
    for r in range(0, src.shape[0], CHUNK):
        k = jnp.exp2(jnp.dot(src[r : r + CHUNK], tgt, preferred_element_type=f32))
        hi = k.astype(bf16)
        at = (slice(row + r, row + r + CHUNK), slice(col, col + tgt.shape[1]))
        k_hi[at] = hi
        k_lo[at] = (k - hi.astype(f32)).astype(bf16)


def times_kernel(v2, k_hi, k_lo, contract=0):
    half = v2.shape[0] // 2
    dims = (((1,), (contract,)), ((), ()))
    r = lax.dot_general(v2, k_hi, dims, preferred_element_type=f32)
    q = lax.dot_general(v2[:half], k_lo, dims, preferred_element_type=f32)
    return r[:half] + r[half:] + q


def repeat(number, step):
    if number <= 8:
        for index in range(number):
            step(index)
    else:
        lax.fori_loop(0, number, lambda index, carry: (step(index), carry)[1], 0)


def kernel(
    n_groups, n_blocks, leaf_count, leaf_size, rank, slots,
    points_in, charges_in, morton_in, neighbours_in, counts_in, skel_leaf_in, skel_block_in, skel_group_in,
    out,
    points, charges, morton, neighbours, counts, skel_leaf, skel_block, skel_group,
    pad_pts, pad_leaf, pad_grp, halo_out, halo_left, halo_right, skel_all, bw_all, gw_all,
    ext_src, ext_c, own_tgt, leaf_src, leaf_tgt, two_tgt,
    kp_hi, kp_lo, kl_hi, kl_lo, kb_hi, kb_lo, kg_hi, kg_lo, kn_hi, kn_lo,
    in_sem, halo_send, halo_recv, skel_send, skel_recv, bw_send, bw_recv, gw_send, gw_recv,
):
    vectors, block_pts = charges.shape
    g = lax.axis_index("grp")
    m = lax.axis_index("dev")
    block = g * n_blocks + m
    total = n_groups * n_blocks
    right = lax.rem(block + 1, total)
    left = lax.rem(block + total - 1, total)
    right_id = (right // n_blocks, lax.rem(right, n_blocks))
    left_id = (left // n_blocks, lax.rem(left, n_blocks))
    peers = [(g, lax.rem(m + d, n_blocks)) for d in range(1, n_blocks)]
    cousins = [(lax.rem(g + d, n_groups), m) for d in range(1, n_groups)]

    barrier = pltpu.get_barrier_semaphore()
    greeted = [left_id, right_id] + peers + cousins
    for who in greeted:
        pl.semaphore_signal(barrier, inc=1, device_id=who, device_id_type=MESH)

    pairs = [
        (skel_block_in, skel_block), (skel_leaf_in, skel_leaf), (morton_in, morton), (points_in, points),
        (charges_in, charges), (skel_group_in, skel_group), (neighbours_in, neighbours), (counts_in, counts),
    ]
    loads = [pltpu.make_async_copy(a, b, in_sem.at[k]) for k, (a, b) in enumerate(pairs)]
    for c in loads:
        c.start()

    def scale(terms):
        return gain_factor / math.sqrt(terms)

    for p in (pad_pts, pad_leaf, pad_grp):
        p[...] = jnp.zeros_like(p)
    skel_all[pl.ds(m, 1)] = jnp.zeros((1, ROWS, rank), f32)

    loads[0].wait()
    skel_all[pl.ds(m, 1), 0:3] = skel_block[...][None]
    loads[1].wait()
    pad_leaf[0:3] = skel_leaf[...]
    _, tgt = features(skel_all[pl.ds(m, 1)][0])
    two_tgt[:, rank:] = tgt.astype(bf16)
    src, tgt = features(pad_leaf[...])
    leaf_src[...] = src.T.astype(bf16)
    leaf_tgt[...] = tgt.astype(bf16)
    fill_kernel(leaf_src[...], two_tgt[:, rank:], kl_hi, kl_lo, 0, 0)

    for c in loads[2:5]:
        c.wait()
    pad_pts[0:3] = points[...]
    pts = pad_pts[...]
    stacked = jnp.concatenate(
        parts(pts, 3) + [jnp.zeros_like(pts)] + parts(charges[...], 2), axis=0
    ).astype(bf16)
    place = lax.broadcasted_iota(jnp.int32, (leaf_size, leaf_size), 0)
    for i in range(leaf_count):
        cols = slice(i * leaf_size, (i + 1) * leaf_size)
        s = jnp.zeros((stacked.shape[0], leaf_size), f32)
        for r in range(0, block_pts, leaf_size):
            onehot = jnp.where(place == morton[0:1, cols] - r, 1.0, 0.0).astype(bf16)
            s = s + jnp.dot(stacked[:, r : r + leaf_size], onehot, preferred_element_type=f32)
        halo_out[0:ROWS, cols] = s[0:8] + s[8:16] + s[16:24]
        halo_out[ROWS:, cols] = s[32 : 32 + vectors] + s[32 + vectors :]

    pl.semaphore_wait(barrier, len(greeted))

    def to_peer(buf, send, recv, k, who, slot):
        return pltpu.make_async_remote_copy(
            src_ref=buf.at[slot], dst_ref=buf.at[slot],
            send_sem=send.at[k], recv_sem=recv.at[slot],
            device_id=who, device_id_type=MESH,
        )

    skel_copies = [to_peer(skel_all, skel_send, skel_recv, k, who, m) for k, who in enumerate(peers)]
    for c in skel_copies:
        c.start()
    halo_copies = [
        pltpu.make_async_remote_copy(
            src_ref=halo_out, dst_ref=dst, send_sem=halo_send.at[k], recv_sem=halo_recv.at[k],
            device_id=who, device_id_type=MESH,
        )
        for k, (dst, who) in enumerate([(halo_left, right_id), (halo_right, left_id)])
    ]
    for c in halo_copies:
        c.start()

    src, tgt = features(halo_out[0:ROWS])
    ext_src[block_pts : 2 * block_pts] = src.T.astype(bf16)
    own_tgt[...] = tgt.astype(bf16)
    ext_c[:, block_pts : 2 * block_pts] = halo_out[ROWS:]
    leaf_w = []
    for i in range(leaf_count):
        pc = slice(i * leaf_size, (i + 1) * leaf_size)
        kc = slice(i * rank, (i + 1) * rank)
        fill_kernel(ext_src[block_pts + i * leaf_size : block_pts + (i + 1) * leaf_size], leaf_tgt[:, kc], kp_hi, kp_lo, i * leaf_size, 0)
        leaf_w.append(times_kernel(split_rows(halo_out[ROWS:, pc]), kp_hi[pc], kp_lo[pc]) * scale(leaf_size))
    lw = jnp.concatenate(leaf_w, axis=1)
    bw_all[pl.ds(m, 1)] = (times_kernel(split_rows(lw), kl_hi[...], kl_lo[...]) * scale(leaf_count * rank))[None]
    bw_copies = [to_peer(bw_all, bw_send, bw_recv, k, who, m) for k, who in enumerate(peers)]
    for c in bw_copies:
        c.start()

    loads[5].wait()
    pad_grp[0:3] = skel_group[...]
    src, tgt = features(pad_grp[...])
    grp_src = src.T.astype(bf16)
    for j in range(n_groups):
        pl.when(g == j)(functools.partial(
            two_tgt.__setitem__, (slice(None), slice(0, rank)), tgt[:, j * rank : (j + 1) * rank].astype(bf16)))
    for j, c in enumerate(peers):
        to_peer(skel_all, skel_send, skel_recv, j, c, c[1]).wait_recv()

    def from_block(b):
        src, _ = features(skel_all[b])
        fill_kernel(src.T.astype(bf16), two_tgt[...], kb_hi.at[b], kb_lo.at[b], 0, 0)

    repeat(n_blocks, from_block)

    for j, c in enumerate(peers):
        to_peer(bw_all, bw_send, bw_recv, j, c, c[1]).wait_recv()

    def add_block(b, carry):
        gw, field = carry
        r = times_kernel(split_rows(bw_all[b]), kb_hi[b], kb_lo[b])
        keep = jnp.where(b == m, 0.0, 1.0)
        return gw + r[:, :rank], field + keep * r[:, rank:]

    empty = jnp.zeros((vectors, rank), f32)
    gw, field = lax.fori_loop(0, n_blocks, add_block, (empty, empty), unroll=True if n_blocks <= 8 else 1)
    field = field * scale((n_blocks - 1) * rank)
    gw_all[pl.ds(g, 1)] = (gw * scale(n_blocks * rank))[None]
    gw_copies = [to_peer(gw_all, gw_send, gw_recv, k, who, g) for k, who in enumerate(cousins)]
    for c in gw_copies:
        c.start()

    fill_kernel(grp_src, two_tgt[:, :rank], kg_hi, kg_lo, 0, 0)

    for c, buf, base in zip(halo_copies, (halo_left, halo_right), (0, 2 * block_pts)):
        c.wait_recv()
        src, _ = features(buf[0:ROWS])
        ext_src[base : base + block_pts] = src.T.astype(bf16)
        ext_c[:, base : base + block_pts] = buf[ROWS:]
    loads[6].wait()
    loads[7].wait()
    first_leaf = block * leaf_count - leaf_count
    window = 2 * leaf_count + 1
    near = []
    for i in range(leaf_count):
        span = slice(i * leaf_size, (i + window) * leaf_size)
        fill_kernel(ext_src[span], own_tgt[:, i * leaf_size : (i + 1) * leaf_size], kn_hi.at[i], kn_lo.at[i], 0, 0)
        values = []
        for o in range(window):
            e = i + o
            piece = ext_c[:, e * leaf_size : (e + 1) * leaf_size]
            if o != leaf_count:
                times = jnp.int32(0)
                for k in range(slots):
                    hit = (neighbours[i, k] - first_leaf == e) & (k < counts[i])
                    times = times + jnp.where(hit, 1, 0)
                piece = piece * times.astype(f32)
            values.append(piece)
        near.append(times_kernel(split_rows(jnp.concatenate(values, axis=1)), kn_hi[i], kn_lo[i]))

    for j, c in enumerate(cousins):
        to_peer(gw_all, gw_send, gw_recv, j, c, c[0]).wait_recv()

    def add_group(h, acc):
        rows = pl.ds(pl.multiple_of(h * rank, rank), rank)
        keep = jnp.where(h == g, 0.0, 1.0)
        return acc + keep * times_kernel(split_rows(gw_all[h]), kg_hi[rows], kg_lo[rows])

    gfield = lax.fori_loop(0, n_groups, add_group, empty, unroll=True if n_groups <= 8 else 1)
    gfield = gfield * scale((n_groups - 1) * rank)
    down_hi = kb_hi[pl.ds(m, 1), :, 0:rank][0]
    down_lo = kb_lo[pl.ds(m, 1), :, 0:rank][0]
    field = field + scale(rank) * times_kernel(split_rows(gfield), down_hi, down_lo, 1)
    lf = times_kernel(split_rows(field), kl_hi[...], kl_lo[...], 1) * scale(rank)
    for i in range(leaf_count):
        pc = slice(i * leaf_size, (i + 1) * leaf_size)
        far = times_kernel(split_rows(lf[:, i * rank : (i + 1) * rank]), kp_hi[pc], kp_lo[pc], 1)
        out[:, pc] = near[i] * scale(leaf_size) + far * scale(rank)

    for c in skel_copies + halo_copies + bw_copies + gw_copies:
        c.wait_send()


def body(n_groups, n_blocks, points, charges, morton, neighbours, counts, skel_leaf, skel_block, skel_group):
    vectors, block_pts = charges.shape
    leaf_count = counts.shape[0]
    leaf_size = block_pts // leaf_count
    rank = skel_block.shape[1]
    slots = neighbours.shape[1]
    leaf_cols = leaf_count * rank
    window = (2 * leaf_count + 1) * leaf_size
    dma = pltpu.SemaphoreType.DMA
    morton = morton.reshape(1, block_pts)
    operands = (points, charges, morton, neighbours, counts, skel_leaf, skel_block, skel_group)
    places = (pltpu.VMEM,) * 3 + (pltpu.SMEM,) * 2 + (pltpu.VMEM,) * 3
    both = lambda *shape: [pltpu.VMEM(shape, bf16)] * 2
    return pl.pallas_call(
        functools.partial(kernel, n_groups, n_blocks, leaf_count, leaf_size, rank, slots),
        out_shape=jax.ShapeDtypeStruct((vectors, block_pts), f32),
        in_specs=[pl.BlockSpec(memory_space=pltpu.HBM)] * len(operands),
        out_specs=pl.BlockSpec(memory_space=pltpu.VMEM),
        scratch_shapes=[
            *[place(a.shape, a.dtype) for place, a in zip(places, operands)],
            pltpu.VMEM((ROWS, block_pts), f32),
            pltpu.VMEM((ROWS, leaf_cols), f32),
            pltpu.VMEM((ROWS, n_groups * rank), f32),
            pltpu.VMEM((ROWS + vectors, block_pts), f32),
            pltpu.VMEM((ROWS + vectors, block_pts), f32),
            pltpu.VMEM((ROWS + vectors, block_pts), f32),
            pltpu.VMEM((n_blocks, ROWS, rank), f32),
            pltpu.VMEM((n_blocks, vectors, rank), f32),
            pltpu.VMEM((n_groups, vectors, rank), f32),
            pltpu.VMEM((3 * block_pts, FEAT), bf16),
            pltpu.VMEM((vectors, 3 * block_pts), f32),
            pltpu.VMEM((FEAT, block_pts), bf16),
            pltpu.VMEM((leaf_cols, FEAT), bf16),
            pltpu.VMEM((FEAT, leaf_cols), bf16),
            pltpu.VMEM((FEAT, 2 * rank), bf16),
            *both(block_pts, rank),
            *both(leaf_cols, rank),
            *both(n_blocks, rank, 2 * rank),
            *both(n_groups * rank, rank),
            *both(leaf_count, window, leaf_size),
            dma((len(operands),)),
            dma((2,)),
            dma((2,)),
            dma((n_blocks - 1,)),
            dma((n_blocks,)),
            dma((n_blocks - 1,)),
            dma((n_blocks,)),
            dma((n_groups - 1,)),
            dma((n_groups,)),
        ],
        compiler_params=pltpu.CompilerParams(
            collective_id=0, has_side_effects=True, vmem_limit_bytes=48 * 1024 * 1024
        ),
    )(*operands)


def solution(mesh):
    return jax.shard_map(
        functools.partial(body, mesh.shape["grp"], mesh.shape["dev"]),
        mesh=mesh,
        in_specs=(
            P(None, ("grp", "dev")),
            P(None, ("grp", "dev")),
            P(("grp", "dev")),
            P(("grp", "dev"), None),
            P(("grp", "dev")),
            P(None, ("grp", "dev")),
            P(None, ("grp", "dev")),
            P(),
        ),
        out_specs=P(None, ("grp", "dev")),
        check_vma=False,
    )
```

time: 30.8 us -> 26.1 us (0.85)
  Pallas kernels: 24 us -> 19.3 us
    pallas_call x1, Pallas kernels: 24 us -> 19.3 us  [body(): pl.pallas_call(functools.partial(kernel, n_groups, n_blocks, leaf_count,...]
where the time goes in v2:
time: 26.1 us; the launch traced here: 25.6 us
  Pallas kernels  19.3 us (74%)
  local copies, waits for them, and re-layouts  6.33 us (24%)
    pallas_call x1, Pallas kernels, body(): pl.pallas_call(functools.partial(kernel, n_groups, n_blocks, leaf_count,...  19.3 us
    unnamed x17, local copies, waits for them, and re-layouts  6.33 us

profile of v2, /device:TPU:0, one launch (start us, length us, event | category | flops | bytes accessed | tf_op | source)
XLA Modules:
  0.0 25.6 jit_solution(18205878804930795700)
XLA Ops:
  0.0 0.0 copy-start.7
  0.0 0.7 %copy-done.7 = s32[4]{0:T(128)S(1)} copy-done((s32[4]{0:T(128)S(1)}, s32[4]{0:T(128)}, u32[]{:S(2)}) %copy-start.7) | copy-done | bytes 40
  0.7 0.0 copy-start
  0.7 0.8 %copy-done = f32[16,1024]{1,0:T(8,128)S(1)} copy-done((f32[16,1024]{1,0:T(8,128)S(1)}, f32[16,1024]{1,0:T(8,128)}, u32[]{:S(2)}) %copy-start) | copy-done | bytes 65560
  1.5 0.0 copy-start.1
  1.5 0.7 %copy-done.1 = f32[3,1024]{1,0:T(4,128)S(1)} copy-done((f32[3,1024]{1,0:T(4,128)S(1)}, f32[3,1024]{1,0:T(4,128)}, u32[]{:S(2)}) %copy-start.1) | copy-done | bytes 12312
  2.2 0.0 copy-start.2
  2.2 0.7 %copy-done.2 = f32[3,1024]{1,0:T(4,128)S(1)} copy-done((f32[3,1024]{1,0:T(4,128)S(1)}, f32[3,1024]{1,0:T(4,128)}, u32[]{:S(2)}) %copy-start.2) | copy-done | bytes 12312
  2.9 0.0 copy-start.3
  2.9 0.7 %copy-done.3 = f32[3,1024]{1,0:T(4,128)S(1)} copy-done((f32[3,1024]{1,0:T(4,128)S(1)}, f32[3,1024]{1,0:T(4,128)}, u32[]{:S(2)}) %copy-start.3) | copy-done | bytes 12312
  3.6 0.0 copy-start.4
  3.7 0.7 %copy-done.4 = s32[1024]{0:T(1024)S(1)} copy-done((s32[1024]{0:T(1024)S(1)}, s32[1024]{0:T(1024)}, u32[]{:S(2)}) %copy-start.4) | copy-done | bytes 4120
  4.3 0.0 copy-start.5
  4.3 0.7 %copy-done.5 = f32[3,256]{1,0:T(4,128)S(1)} copy-done((f32[3,256]{1,0:T(4,128)S(1)}, f32[3,256]{1,0:T(4,128)}, u32[]{:S(2)}) %copy-start.5) | copy-done | bytes 3096
  5.0 0.0 copy-start.6
  5.0 0.7 %copy-done.6 = s32[4,8]{1,0:T(4,128)S(1)} copy-done((s32[4,8]{1,0:T(4,128)S(1)}, s32[4,8]{1,0:T(4,128)}, u32[]{:S(2)}) %copy-start.6) | copy-done | bytes 152
  5.7 19.3 %shard_map.82 = f32[16,1024]{1,0:T(8,128)S(1)} custom-call(f32[3,1024]{1,0:T(4,128)S(1)} %copy-done.1, f32[16,1024]{1,0:T(8,128)S(1)} %copy-done, s32[1,1024]{1,0:T(1,128)S(1)} %bitcast.1, s32[4,8]{1,0:T(4,128)S(1)} %copy-done.6, s32[4]{0:T(128)S(1)} %copy-done.7, f32[3,1024]{1,0:T(4,128)S(1)} %copy-done.2, f32[3,256]{1,0:T(4,128)S(1)} %copy-done.5, ...), custom_call_target="tpu_custom_call" | custom-call | tf_op jit(solution)/shard_map/pallas_call | solution.py:285
  25.0 0.6 %copy.10 = f32[16,1024]{1,0:T(8,128)} copy(f32[16,1024]{1,0:T(8,128)S(1)} %shard_map.82) | data formatting | bytes 131072
Async XLA Ops:
  0.0 0.7 %copy-start.7 = (s32[4]{0:T(128)S(1)}, s32[4]{0:T(128)}, u32[]{:S(2)}) copy-start(s32[4]{0:T(128)} %counts_in.1) | copy-start | bytes 52
  0.7 0.8 %copy-start = (f32[16,1024]{1,0:T(8,128)S(1)}, f32[16,1024]{1,0:T(8,128)}, u32[]{:S(2)}) copy-start(f32[16,1024]{1,0:T(8,128)} %charges_in.1) | copy-start | bytes 196612
  1.5 0.7 %copy-start.1 = (f32[3,1024]{1,0:T(4,128)S(1)}, f32[3,1024]{1,0:T(4,128)}, u32[]{:S(2)}) copy-start(f32[3,1024]{1,0:T(4,128)} %points_in.1) | copy-start | bytes 36868
  2.2 0.7 %copy-start.2 = (f32[3,1024]{1,0:T(4,128)S(1)}, f32[3,1024]{1,0:T(4,128)}, u32[]{:S(2)}) copy-start(f32[3,1024]{1,0:T(4,128)} %skel_leaf_in.1) | copy-start | bytes 36868
  2.9 0.7 %copy-start.3 = (f32[3,1024]{1,0:T(4,128)S(1)}, f32[3,1024]{1,0:T(4,128)}, u32[]{:S(2)}) copy-start(f32[3,1024]{1,0:T(4,128)} %skel_group_in.1) | copy-start | bytes 36868
  3.6 0.7 %copy-start.4 = (s32[1024]{0:T(1024)S(1)}, s32[1024]{0:T(1024)}, u32[]{:S(2)}) copy-start(s32[1024]{0:T(1024)} %param.10) | copy-start | bytes 12292
  4.3 0.7 %copy-start.5 = (f32[3,256]{1,0:T(4,128)S(1)}, f32[3,256]{1,0:T(4,128)}, u32[]{:S(2)}) copy-start(f32[3,256]{1,0:T(4,128)} %skel_block_in.1) | copy-start | bytes 9220
  5.0 0.7 %copy-start.6 = (s32[4,8]{1,0:T(4,128)S(1)}, s32[4,8]{1,0:T(4,128)}, u32[]{:S(2)}) copy-start(s32[4,8]{1,0:T(4,128)} %neighbours_in.1) | copy-start | bytes 388

commit v3 on v2

v3 whole, which is shorter than its diff:
```python
import functools
import math

import jax
import jax.numpy as jnp
from jax import lax
from jax.experimental import pallas as pl
from jax.experimental.pallas import tpu as pltpu
from jax.sharding import PartitionSpec as P

width_sq = 0.1
gain_factor = 5.0
to_base_two = math.sqrt(math.log2(math.e) / width_sq)
middle = 1.0
FEAT = 64
ROWS = 8
MESH = pl.DeviceIdType.MESH
f32, bf16 = jnp.float32, jnp.bfloat16


def parts(x, count):
    out = []
    for _ in range(count - 1):
        out.append(x.astype(bf16).astype(f32))
        x = x - out[-1]
    out.append(x.astype(bf16).astype(f32))
    return out


def features(coords):
    row = lax.broadcasted_iota(jnp.int32, coords.shape, 0)
    c = jnp.where(row < 3, (coords - middle) * to_base_two, 0.0)
    norm = jnp.broadcast_to(jnp.sum(c * c, axis=0, keepdims=True), c.shape)
    hi, mid, lo = parts(c, 3)
    n0, n1, n2 = parts(norm, 3)
    one = jnp.ones_like(c)
    zero = jnp.zeros_like(c)
    first = jnp.where(row == 0, n0, jnp.where(row == 1, n1, n2))
    second = jnp.where(row == 3, n0, jnp.where(row == 4, n1, n2))
    src_n = jnp.where(row < 3, first, jnp.where(row < 6, one, zero))
    tgt_n = jnp.where(row < 3, -one, jnp.where(row < 6, -second, zero))
    hi2, mid2, lo2 = hi + hi, mid + mid, lo + lo
    src = jnp.concatenate([hi, hi, mid, mid, hi, lo, src_n, zero], axis=0)
    tgt = jnp.concatenate([hi2, mid2, hi2, mid2, lo2, hi2, tgt_n, zero], axis=0)
    return src, tgt


def split_rows(v):
    return jnp.concatenate(parts(v, 2), axis=0).astype(bf16)


CHUNK = 64


def fill_kernel(src, tgt, k_hi, k_lo, row, col):
    for r in range(0, src.shape[0], CHUNK):
        k = jnp.exp2(jnp.dot(src[r : r + CHUNK], tgt, preferred_element_type=f32))
        hi = k.astype(bf16)
        at = (slice(row + r, row + r + CHUNK), slice(col, col + tgt.shape[1]))
        k_hi[at] = hi
        k_lo[at] = (k - hi.astype(f32)).astype(bf16)


def times_kernel(v2, k_hi, k_lo, contract=0):
    half = v2.shape[0] // 2
    dims = (((1,), (contract,)), ((), ()))
    r = lax.dot_general(v2, k_hi, dims, preferred_element_type=f32)
    q = lax.dot_general(v2[:half], k_lo, dims, preferred_element_type=f32)
    return r[:half] + r[half:] + q


def repeat(number, step):
    if number <= 8:
        for index in range(1, number):
            step(index)
    else:
        lax.fori_loop(1, number, lambda index, carry: (step(index), carry)[1], 0)


def gather_terms(number, step, start):
    if number <= 8:
        for index in range(1, number):
            start = step(index, start)
        return start
    return lax.fori_loop(1, number, step, start)


def kernel(
    n_groups, n_blocks, leaf_count, leaf_size, rank, slots,
    points_in, charges_in, morton_in, neighbours_in, counts_in, skel_leaf_in, skel_block_in, skel_group_in,
    out,
    points, charges, morton, neighbours, counts, skel_leaf, skel_block, skel_group,
    pad_pts, pad_leaf, pad_grp, halo_out, halo_left, halo_right, msg, gw_all,
    ext_src, ext_c, own_tgt, leaf_src, leaf_tgt, grp_src, grp_tgt, blk_tgt,
    kp_hi, kp_lo, kl_hi, kl_lo, kr_hi, kr_lo, kb_hi, kb_lo, kg_hi, kg_lo, kn_hi, kn_lo,
    in_sem, halo_send, halo_recv, msg_send, msg_recv, gw_send, gw_recv,
):
    vectors, block_pts = charges.shape
    g = lax.axis_index("grp")
    m = lax.axis_index("dev")
    block = g * n_blocks + m
    total = n_groups * n_blocks
    right = lax.rem(block + 1, total)
    left = lax.rem(block + total - 1, total)
    right_id = (right // n_blocks, lax.rem(right, n_blocks))
    left_id = (left // n_blocks, lax.rem(left, n_blocks))
    peers = [(g, lax.rem(m + d, n_blocks)) for d in range(1, n_blocks)]
    cousins = [(lax.rem(g + d, n_groups), m) for d in range(1, n_groups)]

    barrier = pltpu.get_barrier_semaphore()
    greeted = [left_id, right_id] + peers + cousins
    for who in greeted:
        pl.semaphore_signal(barrier, inc=1, device_id=who, device_id_type=MESH)

    pairs = [
        (skel_block_in, skel_block), (skel_leaf_in, skel_leaf), (skel_group_in, skel_group), (morton_in, morton),
        (points_in, points), (charges_in, charges), (neighbours_in, neighbours), (counts_in, counts),
    ]
    loads = [pltpu.make_async_copy(a, b, in_sem.at[k]) for k, (a, b) in enumerate(pairs)]
    for c in loads:
        c.start()

    def scale(terms):
        return gain_factor / math.sqrt(terms)

    def leaf_cols(i):
        return slice(i * leaf_size, (i + 1) * leaf_size)

    def rank_cols(i):
        return slice(i * rank, (i + 1) * rank)

    for p in (pad_pts, pad_leaf, pad_grp):
        p[...] = jnp.zeros_like(p)
    own = pl.ds(m, 1)
    bw_rows = slice(ROWS, ROWS + vectors)
    up_rows = slice(ROWS + vectors, ROWS + 2 * vectors)
    msg[own, 0:ROWS] = jnp.zeros((1, ROWS, rank), f32)

    loads[0].wait()
    msg[own, 0:3] = skel_block[...][None]
    loads[1].wait()
    pad_leaf[0:3] = skel_leaf[...]
    src_b, tgt = features(msg[own, 0:ROWS][0])
    blk_tgt[...] = tgt.astype(bf16)
    src, tgt = features(pad_leaf[...])
    leaf_src[...] = src.T.astype(bf16)
    leaf_tgt[...] = tgt.astype(bf16)
    fill_kernel(leaf_src[...], blk_tgt[...], kl_hi, kl_lo, 0, 0)
    loads[2].wait()
    pad_grp[0:3] = skel_group[...]
    src, tgt = features(pad_grp[...])
    grp_src[...] = src.T.astype(bf16)
    for j in range(n_groups):
        pl.when(g == j)(functools.partial(
            grp_tgt.__setitem__, (slice(None), slice(None)), tgt[:, rank_cols(j)].astype(bf16)))
    fill_kernel(src_b.T.astype(bf16), grp_tgt[...], kr_hi, kr_lo, 0, 0)

    for c in loads[3:6]:
        c.wait()
    pad_pts[0:3] = points[...]
    pts = pad_pts[...]
    stacked = jnp.concatenate(
        parts(pts, 3) + [jnp.zeros_like(pts)] + parts(charges[...], 2), axis=0
    ).astype(bf16)
    place = lax.broadcasted_iota(jnp.int32, (leaf_size, leaf_size), 0)
    for i in range(leaf_count):
        s = jnp.zeros((stacked.shape[0], leaf_size), f32)
        for r in range(0, block_pts, leaf_size):
            onehot = jnp.where(place == morton[0:1, leaf_cols(i)] - r, 1.0, 0.0).astype(bf16)
            s = s + jnp.dot(stacked[:, r : r + leaf_size], onehot, preferred_element_type=f32)
        halo_out[0:ROWS, leaf_cols(i)] = s[0:8] + s[8:16] + s[16:24]
        halo_out[ROWS:, leaf_cols(i)] = s[32 : 32 + vectors] + s[32 + vectors :]

    src, tgt = features(halo_out[0:ROWS])
    ext_src[block_pts : 2 * block_pts] = src.T.astype(bf16)
    own_tgt[...] = tgt.astype(bf16)
    leaf_w = []
    for i in range(leaf_count):
        fill_kernel(ext_src[leaf_cols(leaf_count + i)], leaf_tgt[:, rank_cols(i)], kp_hi, kp_lo, i * leaf_size, 0)
        leaf_w.append(times_kernel(split_rows(halo_out[ROWS:, leaf_cols(i)]), kp_hi[leaf_cols(i)], kp_lo[leaf_cols(i)]))
    lw = jnp.concatenate(leaf_w, axis=1) * scale(leaf_size)
    bw = times_kernel(split_rows(lw), kl_hi[...], kl_lo[...]) * scale(leaf_count * rank)
    msg[own, bw_rows] = bw[None]
    msg[own, up_rows] = (times_kernel(split_rows(bw), kr_hi[...], kr_lo[...]) * scale(n_blocks * rank))[None]

    pl.semaphore_wait(barrier, len(greeted))

    def to_peer(buf, send, recv, k, who, slot):
        return pltpu.make_async_remote_copy(
            src_ref=buf.at[slot], dst_ref=buf.at[slot],
            send_sem=send.at[k], recv_sem=recv.at[slot],
            device_id=who, device_id_type=MESH,
        )

    msg_copies = [to_peer(msg, msg_send, msg_recv, k, who, m) for k, who in enumerate(peers)]
    halo_copies = [
        pltpu.make_async_remote_copy(
            src_ref=halo_out, dst_ref=dst, send_sem=halo_send.at[k], recv_sem=halo_recv.at[k],
            device_id=who, device_id_type=MESH,
        )
        for k, (dst, who) in enumerate([(halo_left, right_id), (halo_right, left_id)])
    ]
    for c in msg_copies + halo_copies:
        c.start()

    ext_c[:, block_pts : 2 * block_pts] = halo_out[ROWS:]
    loads[6].wait()
    loads[7].wait()
    first_leaf = block * leaf_count - leaf_count

    def values(i, e):
        piece = ext_c[:, leaf_cols(e)]
        if e == leaf_count + i:
            return piece
        times = jnp.int32(0)
        for k in range(slots):
            hit = (neighbours[i, k] - first_leaf == e) & (k < counts[i])
            times = times + jnp.where(hit, 1, 0)
        return piece * times.astype(f32)

    def joined(pieces):
        return split_rows(jnp.concatenate(pieces, axis=1))

    near = []
    for i in range(leaf_count):
        rows = (i + 1) * leaf_size
        fill_kernel(
            ext_src[block_pts : block_pts + rows], own_tgt[:, leaf_cols(i)], kn_hi.at[i], kn_lo.at[i], 0, 0)
    for i in range(leaf_count):
        rows = (i + 1) * leaf_size
        v2 = joined([values(i, leaf_count + j) for j in range(i + 1)])
        acc = times_kernel(v2, kn_hi[i, 0:rows], kn_lo[i, 0:rows])
        for j in range(i + 1, leaf_count):
            acc = acc + times_kernel(
                split_rows(values(i, leaf_count + j)), kn_hi[j, leaf_cols(i)], kn_lo[j, leaf_cols(i)], 1)
        near.append(acc)

    for j, c in enumerate(peers):
        to_peer(msg, msg_send, msg_recv, j, c, c[1]).wait_recv()
    gw_all[pl.ds(g, 1)] = jnp.sum(msg[:, up_rows], axis=0, keepdims=True)
    gw_copies = [to_peer(gw_all, gw_send, gw_recv, k, who, g) for k, who in enumerate(cousins)]
    for c in gw_copies:
        c.start()

    empty = jnp.zeros((vectors, rank), f32)

    def cousin_rows(d):
        return pl.ds(pl.multiple_of(lax.rem(g + d, n_groups) * rank, rank), rank)

    def fill_group(d):
        fill_kernel(grp_src[cousin_rows(d)], grp_tgt[...], kg_hi.at[d - 1], kg_lo.at[d - 1], 0, 0)

    def fill_peer(d):
        src, _ = features(msg[lax.rem(m + d, n_blocks), 0:ROWS])
        fill_kernel(src.T.astype(bf16), blk_tgt[...], kb_hi.at[d - 1], kb_lo.at[d - 1], 0, 0)

    def add_peer(d, acc):
        v2 = split_rows(msg[lax.rem(m + d, n_blocks), bw_rows])
        return acc + times_kernel(v2, kb_hi[d - 1], kb_lo[d - 1])

    repeat(n_groups, fill_group)
    repeat(n_blocks, fill_peer)
    field = gather_terms(n_blocks, add_peer, empty) * scale((n_blocks - 1) * rank)

    for c, buf, base in zip(halo_copies, (halo_left, halo_right), (0, 2 * block_pts)):
        c.wait_recv()
        src, _ = features(buf[0:ROWS])
        ext_src[base : base + block_pts] = src.T.astype(bf16)
        ext_c[:, base : base + block_pts] = buf[ROWS:]
    for i in range(leaf_count):
        base = leaf_count * leaf_size
        before = list(range(i, leaf_count))
        after = list(range(2 * leaf_count, 2 * leaf_count + i + 1))
        split = base + len(before) * leaf_size
        end = split + len(after) * leaf_size
        target = own_tgt[:, leaf_cols(i)]
        fill_kernel(ext_src[i * leaf_size : block_pts], target, kn_hi.at[i], kn_lo.at[i], base, 0)
        fill_kernel(
            ext_src[2 * block_pts : 2 * block_pts + len(after) * leaf_size], target, kn_hi.at[i], kn_lo.at[i], split, 0)
        v2 = joined([values(i, e) for e in before + after])
        near[i] = near[i] + times_kernel(v2, kn_hi[i, base:end], kn_lo[i, base:end])

    for j, c in enumerate(cousins):
        to_peer(gw_all, gw_send, gw_recv, j, c, c[0]).wait_recv()

    def add_group(d, acc):
        v2 = split_rows(gw_all[lax.rem(g + d, n_groups)])
        return acc + times_kernel(v2, kg_hi[d - 1], kg_lo[d - 1])

    gfield = gather_terms(n_groups, add_group, empty) * scale((n_groups - 1) * rank)
    field = field + scale(rank) * times_kernel(split_rows(gfield), kr_hi[...], kr_lo[...], 1)
    lf = times_kernel(split_rows(field), kl_hi[...], kl_lo[...], 1) * scale(rank)
    for i in range(leaf_count):
        far = times_kernel(split_rows(lf[:, rank_cols(i)]), kp_hi[leaf_cols(i)], kp_lo[leaf_cols(i)], 1)
        out[:, leaf_cols(i)] = near[i] * scale(leaf_size) + far * scale(rank)

    for c in msg_copies + halo_copies + gw_copies:
        c.wait_send()


def body(n_groups, n_blocks, points, charges, morton, neighbours, counts, skel_leaf, skel_block, skel_group):
    vectors, block_pts = charges.shape
    leaf_count = counts.shape[0]
    leaf_size = block_pts // leaf_count
    rank = skel_block.shape[1]
    slots = neighbours.shape[1]
    leaf_cols = leaf_count * rank
    window = (2 * leaf_count + 1) * leaf_size
    dma = pltpu.SemaphoreType.DMA
    morton = morton.reshape(1, block_pts)
    operands = (points, charges, morton, neighbours, counts, skel_leaf, skel_block, skel_group)
    places = (pltpu.VMEM,) * 3 + (pltpu.SMEM,) * 2 + (pltpu.VMEM,) * 3
    both = lambda *shape: [pltpu.VMEM(shape, bf16)] * 2
    return pl.pallas_call(
        functools.partial(kernel, n_groups, n_blocks, leaf_count, leaf_size, rank, slots),
        out_shape=jax.ShapeDtypeStruct((vectors, block_pts), f32),
        in_specs=[pl.BlockSpec(memory_space=pltpu.HBM)] * len(operands),
        out_specs=pl.BlockSpec(memory_space=pltpu.VMEM),
        scratch_shapes=[
            *[place(a.shape, a.dtype) for place, a in zip(places, operands)],
            pltpu.VMEM((ROWS, block_pts), f32),
            pltpu.VMEM((ROWS, leaf_cols), f32),
            pltpu.VMEM((ROWS, n_groups * rank), f32),
            pltpu.VMEM((ROWS + vectors, block_pts), f32),
            pltpu.VMEM((ROWS + vectors, block_pts), f32),
            pltpu.VMEM((ROWS + vectors, block_pts), f32),
            pltpu.VMEM((n_blocks, ROWS + 2 * vectors, rank), f32),
            pltpu.VMEM((n_groups, vectors, rank), f32),
            pltpu.VMEM((3 * block_pts, FEAT), bf16),
            pltpu.VMEM((vectors, 3 * block_pts), f32),
            pltpu.VMEM((FEAT, block_pts), bf16),
            pltpu.VMEM((leaf_cols, FEAT), bf16),
            pltpu.VMEM((FEAT, leaf_cols), bf16),
            pltpu.VMEM((n_groups * rank, FEAT), bf16),
            pltpu.VMEM((FEAT, rank), bf16),
            pltpu.VMEM((FEAT, rank), bf16),
            *both(block_pts, rank),
            *both(leaf_cols, rank),
            *both(rank, rank),
            *both(n_blocks - 1, rank, rank),
            *both(n_groups - 1, rank, rank),
            *both(leaf_count, window, leaf_size),
            dma((len(operands),)),
            dma((2,)),
            dma((2,)),
            dma((n_blocks - 1,)),
            dma((n_blocks,)),
            dma((n_groups - 1,)),
            dma((n_groups,)),
        ],
        compiler_params=pltpu.CompilerParams(
            collective_id=0, has_side_effects=True, vmem_limit_bytes=64 * 1024 * 1024
        ),
    )(*operands)


def solution(mesh):
    return jax.shard_map(
        functools.partial(body, mesh.shape["grp"], mesh.shape["dev"]),
        mesh=mesh,
        in_specs=(
            P(None, ("grp", "dev")),
            P(None, ("grp", "dev")),
            P(("grp", "dev")),
            P(("grp", "dev"), None),
            P(("grp", "dev")),
            P(None, ("grp", "dev")),
            P(None, ("grp", "dev")),
            P(),
        ),
        out_specs=P(None, ("grp", "dev")),
        check_vma=False,
    )
```

time: 26.1 us -> 22.9 us (0.88); the launches traced: 25.6 us -> 22.7 us
  local copies, waits for them, and re-layouts: 6.33 us -> 1.47 us
  Pallas kernels: 19.3 us -> 21.2 us
    unnamed x17 -> x1, local copies, waits for them, and re-layouts: 6.33 us -> 1.47 us
    pallas_call x1, Pallas kernels: 19.3 us -> 21.2 us  [body(): pl.pallas_call(functools.partial(kernel, n_groups, n_blocks, leaf_count,...]
where the time goes in v3:
time: 22.9 us; the launch traced here: 22.7 us
  Pallas kernels  21.2 us (93%)
  local copies, waits for them, and re-layouts  1.47 us (6%)
    pallas_call x1, Pallas kernels, body(): pl.pallas_call(functools.partial(kernel, n_groups, n_blocks, leaf_count,...  21.2 us
    unnamed x1, local copies, waits for them, and re-layouts  1.47 us

profile of v3, /device:TPU:0, one launch (start us, length us, event | category | flops | bytes accessed | tf_op | source)
XLA Modules:
  0.0 22.7 jit_solution(687498123012551009)
XLA Ops:
  0.0 21.2 %shard_map.82 = f32[16,1024]{1,0:T(8,128)} custom-call(f32[3,1024]{1,0:T(4,128)} %points_in.1, f32[16,1024]{1,0:T(8,128)} %charges_in.1, s32[1,1024]{1,0:T(1,128)} %bitcast.1, s32[4,8]{1,0:T(4,128)} %neighbours_in.1, s32[4]{0:T(128)} %counts_in.1, f32[3,1024]{1,0:T(4,128)} %skel_leaf_in.1, f32[3,256]{1,0:T(4,128)} %skel_block_in.1, f32[3,1024]{1,0:T(4,128)} %skel_group_in.1), custom_call_target="tpu_custom_call" | custom-call | tf_op jit(solution)/shard_map/pallas_call | solution.py:314
  21.3 1.5 %copy.10 = f32[16,1024]{1,0:T(8,128)} copy(f32[16,1024]{1,0:T(8,128)} %shard_map.82) | data formatting | bytes 131072

commit v4 on v3

--- a/solution.py
+++ b/solution.py
@@ -12,8 +12,9 @@
 gain_factor = 5.0
 to_base_two = math.sqrt(math.log2(math.e) / width_sq)
 middle = 1.0
-FEAT = 64
+FEAT = 32
 ROWS = 8
+SENT = 4
 MESH = pl.DeviceIdType.MESH
 f32, bf16 = jnp.float32, jnp.bfloat16
 
@@ -29,19 +30,18 @@
 
 def features(coords):
     row = lax.broadcasted_iota(jnp.int32, coords.shape, 0)
-    c = jnp.where(row < 3, (coords - middle) * to_base_two, 0.0)
-    norm = jnp.broadcast_to(jnp.sum(c * c, axis=0, keepdims=True), c.shape)
+    low, used = row < 3, row < 6
+    c = jnp.where(used, (coords - middle) * to_base_two, 0.0)
+    norm = jnp.sum(jnp.where(low, c * c, 0.0), axis=0, keepdims=True)
+    norm = jnp.broadcast_to(norm, c.shape)
     hi, mid, lo = parts(c, 3)
     n0, n1, n2 = parts(norm, 3)
-    one = jnp.ones_like(c)
-    zero = jnp.zeros_like(c)
-    first = jnp.where(row == 0, n0, jnp.where(row == 1, n1, n2))
-    second = jnp.where(row == 3, n0, jnp.where(row == 4, n1, n2))
-    src_n = jnp.where(row < 3, first, jnp.where(row < 6, one, zero))
-    tgt_n = jnp.where(row < 3, -one, jnp.where(row < 6, -second, zero))
-    hi2, mid2, lo2 = hi + hi, mid + mid, lo + lo
-    src = jnp.concatenate([hi, hi, mid, mid, hi, lo, src_n, zero], axis=0)
-    tgt = jnp.concatenate([hi2, mid2, hi2, mid2, lo2, hi2, tgt_n, zero], axis=0)
+    nth = jnp.where((row == 0) | (row == 3), n0, jnp.where((row == 1) | (row == 4), n1, n2))
+    src_n = jnp.where(low, nth, jnp.where(used, 1.0, 0.0))
+    tgt_n = jnp.where(low, -1.0, jnp.where(used, -nth, 0.0))
+    upper = jnp.where(low, hi + hi, mid + mid)
+    src = jnp.concatenate([hi, mid, jnp.where(low, hi, lo), src_n], axis=0)
+    tgt = jnp.concatenate([upper, upper, jnp.where(low, lo + lo, hi + hi), tgt_n], axis=0)
     return src, tgt
 
 
@@ -90,10 +90,11 @@
     points_in, charges_in, morton_in, neighbours_in, counts_in, skel_leaf_in, skel_block_in, skel_group_in,
     out,
     points, charges, morton, neighbours, counts, skel_leaf, skel_block, skel_group,
-    pad_pts, pad_leaf, pad_grp, halo_out, halo_left, halo_right, msg, gw_all,
+    pad_pts, pad_leaf, pad_grp, pad_blk, pad_left, pad_right, sorted_pts, chg_out, chg_left, chg_right,
+    pts_out, pts_left, pts_right, skel_all, up_out, up_in, bw_all, gw_out, gw_all,
     ext_src, ext_c, own_tgt, leaf_src, leaf_tgt, grp_src, grp_tgt, blk_tgt,
     kp_hi, kp_lo, kl_hi, kl_lo, kr_hi, kr_lo, kb_hi, kb_lo, kg_hi, kg_lo, kn_hi, kn_lo,
-    in_sem, halo_send, halo_recv, msg_send, msg_recv, gw_send, gw_recv,
+    in_sem, halo_send, halo_recv, skel_send, skel_recv, up_send, up_recv, bw_send, bw_recv, gw_send, gw_recv,
 ):
     vectors, block_pts = charges.shape
     g = lax.axis_index("grp")
@@ -105,7 +106,11 @@
     right_id = (right // n_blocks, lax.rem(right, n_blocks))
     left_id = (left // n_blocks, lax.rem(left, n_blocks))
     peers = [(g, lax.rem(m + d, n_blocks)) for d in range(1, n_blocks)]
-    cousins = [(lax.rem(g + d, n_groups), m) for d in range(1, n_groups)]
+    core = lax.rem(m, 2)
+    twin = m + 1 - 2 * core
+    same_core = [lax.rem(m + 2 * d, n_blocks) for d in range(1, n_blocks // 2)]
+    cousins = [(lax.rem(g + d, n_groups), who) for d in range(1, n_groups) for who in (m, twin)]
+    half = vectors // 2
 
     barrier = pltpu.get_barrier_semaphore()
     greeted = [left_id, right_id] + peers + cousins
@@ -129,26 +134,24 @@
     def rank_cols(i):
         return slice(i * rank, (i + 1) * rank)
 
-    for p in (pad_pts, pad_leaf, pad_grp):
-        p[...] = jnp.zeros_like(p)
-    own = pl.ds(m, 1)
-    bw_rows = slice(ROWS, ROWS + vectors)
-    up_rows = slice(ROWS + vectors, ROWS + 2 * vectors)
-    msg[own, 0:ROWS] = jnp.zeros((1, ROWS, rank), f32)
+    def doubled(pad, coords):
+        pad[6:8] = jnp.zeros((2, coords.shape[1]), f32)
+        pad[0:3] = coords
+        pad[3:6] = coords
+        return features(pad[...])
 
     loads[0].wait()
-    msg[own, 0:3] = skel_block[...][None]
+    skel_all[pl.ds(m, 1), 0:3] = skel_block[...][None]
+    skel_all[pl.ds(m, 1), 3:4] = jnp.zeros((1, 1, rank), f32)
+    src_b, tgt = doubled(pad_blk.at[0], skel_block[...])
+    blk_tgt[...] = tgt.astype(bf16)
     loads[1].wait()
-    pad_leaf[0:3] = skel_leaf[...]
-    src_b, tgt = features(msg[own, 0:ROWS][0])
-    blk_tgt[...] = tgt.astype(bf16)
-    src, tgt = features(pad_leaf[...])
+    src, tgt = doubled(pad_leaf, skel_leaf[...])
     leaf_src[...] = src.T.astype(bf16)
     leaf_tgt[...] = tgt.astype(bf16)
     fill_kernel(leaf_src[...], blk_tgt[...], kl_hi, kl_lo, 0, 0)
     loads[2].wait()
-    pad_grp[0:3] = skel_group[...]
-    src, tgt = features(pad_grp[...])
+    src, tgt = doubled(pad_grp, skel_group[...])
     grp_src[...] = src.T.astype(bf16)
     for j in range(n_groups):
         pl.when(g == j)(functools.partial(
@@ -157,7 +160,9 @@
 
     for c in loads[3:6]:
         c.wait()
+    pad_pts[6:8] = jnp.zeros((2, block_pts), f32)
     pad_pts[0:3] = points[...]
+    pad_pts[3:6] = points[...]
     pts = pad_pts[...]
     stacked = jnp.concatenate(
         parts(pts, 3) + [jnp.zeros_like(pts)] + parts(charges[...], 2), axis=0
@@ -168,42 +173,71 @@
         for r in range(0, block_pts, leaf_size):
             onehot = jnp.where(place == morton[0:1, leaf_cols(i)] - r, 1.0, 0.0).astype(bf16)
             s = s + jnp.dot(stacked[:, r : r + leaf_size], onehot, preferred_element_type=f32)
-        halo_out[0:ROWS, leaf_cols(i)] = s[0:8] + s[8:16] + s[16:24]
-        halo_out[ROWS:, leaf_cols(i)] = s[32 : 32 + vectors] + s[32 + vectors :]
-
-    src, tgt = features(halo_out[0:ROWS])
+        sorted_pts[:, leaf_cols(i)] = s[0:8] + s[8:16] + s[16:24]
+        chg_out[:, leaf_cols(i)] = s[32 : 32 + vectors] + s[32 + vectors :]
+    pts_out[...] = sorted_pts[0:SENT]
+
+    def to_peer(src, dst, send, recv, who):
+        return pltpu.make_async_remote_copy(
+            src_ref=src, dst_ref=dst, send_sem=send, recv_sem=recv, device_id=who, device_id_type=MESH)
+
+    def skel_copy(k, who, slot):
+        return to_peer(skel_all.at[slot], skel_all.at[slot], skel_send.at[k], skel_recv.at[slot], who)
+
+    to_right = [
+        to_peer(pts_out, pts_left, halo_send.at[0], halo_recv.at[0], right_id),
+        to_peer(chg_out, chg_left, halo_send.at[1], halo_recv.at[1], right_id),
+    ]
+    to_left = [
+        to_peer(pts_out, pts_right, halo_send.at[2], halo_recv.at[2], left_id),
+        to_peer(chg_out, chg_right, halo_send.at[3], halo_recv.at[3], left_id),
+    ]
+    has_left, has_right = block > 0, block < total - 1
+
+    pl.semaphore_wait(barrier, len(greeted))
+    skel_copies = [skel_copy(k, who, m) for k, who in enumerate(peers)]
+    for c in skel_copies:
+        c.start()
+
+    @pl.when(has_right)
+    def _():
+        for c in to_right:
+            c.start()
+
+    @pl.when(has_left)
+    def _():
+        for c in to_left:
+            c.start()
+
+    src, tgt = features(sorted_pts[...])
     ext_src[block_pts : 2 * block_pts] = src.T.astype(bf16)
     own_tgt[...] = tgt.astype(bf16)
     leaf_w = []
     for i in range(leaf_count):
         fill_kernel(ext_src[leaf_cols(leaf_count + i)], leaf_tgt[:, rank_cols(i)], kp_hi, kp_lo, i * leaf_size, 0)
-        leaf_w.append(times_kernel(split_rows(halo_out[ROWS:, leaf_cols(i)]), kp_hi[leaf_cols(i)], kp_lo[leaf_cols(i)]))
+        leaf_w.append(times_kernel(split_rows(chg_out[:, leaf_cols(i)]), kp_hi[leaf_cols(i)], kp_lo[leaf_cols(i)]))
     lw = jnp.concatenate(leaf_w, axis=1) * scale(leaf_size)
     bw = times_kernel(split_rows(lw), kl_hi[...], kl_lo[...]) * scale(leaf_count * rank)
-    msg[own, bw_rows] = bw[None]
-    msg[own, up_rows] = (times_kernel(split_rows(bw), kr_hi[...], kr_lo[...]) * scale(n_blocks * rank))[None]
-
-    pl.semaphore_wait(barrier, len(greeted))
-
-    def to_peer(buf, send, recv, k, who, slot):
-        return pltpu.make_async_remote_copy(
-            src_ref=buf.at[slot], dst_ref=buf.at[slot],
-            send_sem=send.at[k], recv_sem=recv.at[slot],
-            device_id=who, device_id_type=MESH,
-        )
-
-    msg_copies = [to_peer(msg, msg_send, msg_recv, k, who, m) for k, who in enumerate(peers)]
-    halo_copies = [
-        pltpu.make_async_remote_copy(
-            src_ref=halo_out, dst_ref=dst, send_sem=halo_send.at[k], recv_sem=halo_recv.at[k],
-            device_id=who, device_id_type=MESH,
-        )
-        for k, (dst, who) in enumerate([(halo_left, right_id), (halo_right, left_id)])
-    ]
-    for c in msg_copies + halo_copies:
+    bw_all[pl.ds(m, 1)] = bw[None]
+    up = times_kernel(split_rows(bw), kr_hi[...], kr_lo[...]) * scale(n_blocks * rank)
+    up_out[0] = up[:half]
+    up_out[1] = up[half:]
+
+    def up_copy(k, who, slot):
+        return to_peer(up_out.at[lax.rem(who[1], 2)], up_in.at[slot], up_send.at[k], up_recv.at[slot], who)
+
+    def bw_copy(k, who, slot):
+        return to_peer(bw_all.at[slot], bw_all.at[slot], bw_send.at[k], bw_recv.at[slot], (g, who))
+
+    def gw_copy(k, who, group, part):
+        return to_peer(gw_out, gw_all.at[group, part], gw_send.at[k], gw_recv.at[group, part], who)
+
+    up_copies = [up_copy(k, who, m) for k, who in enumerate(peers)]
+    bw_copies = [bw_copy(k, who, m) for k, who in enumerate([twin] + same_core)]
+    for c in up_copies + bw_copies:
         c.start()
 
-    ext_c[:, block_pts : 2 * block_pts] = halo_out[ROWS:]
+    ext_c[:, block_pts : 2 * block_pts] = chg_out[...]
     loads[6].wait()
     loads[7].wait()
     first_leaf = block * leaf_count - leaf_count
@@ -235,12 +269,19 @@
                 split_rows(values(i, leaf_count + j)), kn_hi[j, leaf_cols(i)], kn_lo[j, leaf_cols(i)], 1)
         near.append(acc)
 
+    gw = up_out[pl.ds(core, 1)][0]
     for j, c in enumerate(peers):
-        to_peer(msg, msg_send, msg_recv, j, c, c[1]).wait_recv()
-    gw_all[pl.ds(g, 1)] = jnp.sum(msg[:, up_rows], axis=0, keepdims=True)
-    gw_copies = [to_peer(gw_all, gw_send, gw_recv, k, who, g) for k, who in enumerate(cousins)]
+        up_copy(j, c, c[1]).wait_recv()
+        gw = gw + up_in[pl.ds(c[1], 1)][0]
+    gw_out[...] = gw
+    gw_copies = [gw_copy(k, who, g, core) for k, who in enumerate(cousins)]
     for c in gw_copies:
         c.start()
+    forwards = []
+    for k, c in enumerate(same_core):
+        bw_copy(0, twin, c).wait_recv()
+        forwards.append(bw_copy(1 + len(same_core) + k, twin, c))
+        forwards[-1].start()
 
     empty = jnp.zeros((vectors, rank), f32)
 
@@ -251,22 +292,35 @@
         fill_kernel(grp_src[cousin_rows(d)], grp_tgt[...], kg_hi.at[d - 1], kg_lo.at[d - 1], 0, 0)
 
     def fill_peer(d):
-        src, _ = features(msg[lax.rem(m + d, n_blocks), 0:ROWS])
+        src, _ = doubled(pad_blk.at[d], skel_all[lax.rem(m + d, n_blocks)][0:3])
         fill_kernel(src.T.astype(bf16), blk_tgt[...], kb_hi.at[d - 1], kb_lo.at[d - 1], 0, 0)
 
     def add_peer(d, acc):
-        v2 = split_rows(msg[lax.rem(m + d, n_blocks), bw_rows])
+        v2 = split_rows(bw_all[lax.rem(m + d, n_blocks)])
         return acc + times_kernel(v2, kb_hi[d - 1], kb_lo[d - 1])
 
     repeat(n_groups, fill_group)
+    for j, c in enumerate(peers):
+        skel_copy(j, c, c[1]).wait_recv()
     repeat(n_blocks, fill_peer)
-    field = gather_terms(n_blocks, add_peer, empty) * scale((n_blocks - 1) * rank)
-
-    for c, buf, base in zip(halo_copies, (halo_left, halo_right), (0, 2 * block_pts)):
-        c.wait_recv()
-        src, _ = features(buf[0:ROWS])
+
+    def halo(there, copies, pts, chg, pad, base):
+        @pl.when(there)
+        def _():
+            for c in copies:
+                c.wait_recv()
+
+        @pl.when(jnp.logical_not(there))
+        def _():
+            pts[...] = jnp.zeros_like(pts)
+            chg[...] = jnp.zeros_like(chg)
+
+        src, _ = doubled(pad, pts[0:3])
         ext_src[base : base + block_pts] = src.T.astype(bf16)
-        ext_c[:, base : base + block_pts] = buf[ROWS:]
+        ext_c[:, base : base + block_pts] = chg[...]
+
+    halo(has_left, to_right, pts_left, chg_left, pad_left, 0)
+    halo(has_right, to_left, pts_right, chg_right, pad_right, 2 * block_pts)
     for i in range(leaf_count):
         base = leaf_count * leaf_size
         before = list(range(i, leaf_count))
@@ -280,11 +334,17 @@
         v2 = joined([values(i, e) for e in before + after])
         near[i] = near[i] + times_kernel(v2, kn_hi[i, base:end], kn_lo[i, base:end])
 
-    for j, c in enumerate(cousins):
-        to_peer(gw_all, gw_send, gw_recv, j, c, c[0]).wait_recv()
+    bw_copy(0, twin, twin).wait_recv()
+    for c in same_core:
+        bw_copy(0, twin, lax.rem(c + twin - m + n_blocks, n_blocks)).wait_recv()
+    field = gather_terms(n_blocks, add_peer, empty) * scale((n_blocks - 1) * rank)
+    for d in range(1, n_groups):
+        for part in range(2):
+            gw_copy(0, cousins[0], lax.rem(g + d, n_groups), part).wait_recv()
 
     def add_group(d, acc):
-        v2 = split_rows(gw_all[lax.rem(g + d, n_groups)])
+        h = lax.rem(g + d, n_groups)
+        v2 = split_rows(jnp.concatenate([gw_all[h, 0], gw_all[h, 1]], axis=0))
         return acc + times_kernel(v2, kg_hi[d - 1], kg_lo[d - 1])
 
     gfield = gather_terms(n_groups, add_group, empty) * scale((n_groups - 1) * rank)
@@ -294,7 +354,17 @@
         far = times_kernel(split_rows(lf[:, rank_cols(i)]), kp_hi[leaf_cols(i)], kp_lo[leaf_cols(i)], 1)
         out[:, leaf_cols(i)] = near[i] * scale(leaf_size) + far * scale(rank)
 
-    for c in msg_copies + halo_copies + gw_copies:
+    @pl.when(has_right)
+    def _():
+        for c in to_right:
+            c.wait_send()
+
+    @pl.when(has_left)
+    def _():
+        for c in to_left:
+            c.wait_send()
+
+    for c in skel_copies + up_copies + bw_copies + forwards + gw_copies:
         c.wait_send()
 
 
@@ -321,11 +391,22 @@
             pltpu.VMEM((ROWS, block_pts), f32),
             pltpu.VMEM((ROWS, leaf_cols), f32),
             pltpu.VMEM((ROWS, n_groups * rank), f32),
-            pltpu.VMEM((ROWS + vectors, block_pts), f32),
-            pltpu.VMEM((ROWS + vectors, block_pts), f32),
-            pltpu.VMEM((ROWS + vectors, block_pts), f32),
-            pltpu.VMEM((n_blocks, ROWS + 2 * vectors, rank), f32),
-            pltpu.VMEM((n_groups, vectors, rank), f32),
+            pltpu.VMEM((n_blocks, ROWS, rank), f32),
+            pltpu.VMEM((ROWS, block_pts), f32),
+            pltpu.VMEM((ROWS, block_pts), f32),
+            pltpu.VMEM((ROWS, block_pts), f32),
+            pltpu.VMEM((vectors, block_pts), f32),
+            pltpu.VMEM((vectors, block_pts), f32),
+            pltpu.VMEM((vectors, block_pts), f32),
+            pltpu.VMEM((SENT, block_pts), f32),
+            pltpu.VMEM((SENT, block_pts), f32),
+            pltpu.VMEM((SENT, block_pts), f32),
+            pltpu.VMEM((n_blocks, SENT, rank), f32),
+            pltpu.VMEM((2, vectors // 2, rank), f32),
+            pltpu.VMEM((n_blocks, vectors // 2, rank), f32),
+            pltpu.VMEM((n_blocks, vectors, rank), f32),
+            pltpu.VMEM((vectors // 2, rank), f32),
+            pltpu.VMEM((n_groups, 2, vectors // 2, rank), f32),
             pltpu.VMEM((3 * block_pts, FEAT), bf16),
             pltpu.VMEM((vectors, 3 * block_pts), f32),
             pltpu.VMEM((FEAT, block_pts), bf16),
@@ -341,12 +422,16 @@
             *both(n_groups - 1, rank, rank),
             *both(leaf_count, window, leaf_size),
             dma((len(operands),)),
-            dma((2,)),
-            dma((2,)),
+            dma((4,)),
+            dma((4,)),
             dma((n_blocks - 1,)),
             dma((n_blocks,)),
-            dma((n_groups - 1,)),
-            dma((n_groups,)),
+            dma((n_blocks - 1,)),
+            dma((n_blocks,)),
+            dma((n_blocks,)),
+            dma((n_blocks,)),
+            dma((2 * (n_groups - 1),)),
+            dma((n_groups, 2)),
         ],
         compiler_params=pltpu.CompilerParams(
             collective_id=0, has_side_effects=True, vmem_limit_bytes=64 * 1024 * 1024

time: 22.9 us -> 20.6 us (0.90)
  Pallas kernels: 21.2 us -> 19 us
    pallas_call x1, Pallas kernels: 21.2 us -> 19 us  [body(): pl.pallas_call(functools.partial(kernel, n_groups, n_blocks, leaf_count,...]
where the time goes in v4:
time: 20.6 us; the launch traced here: 20.4 us
  Pallas kernels  19 us (92%)
  local copies, waits for them, and re-layouts  1.47 us (7%)
    pallas_call x1, Pallas kernels, body(): pl.pallas_call(functools.partial(kernel, n_groups, n_blocks, leaf_count,...  19 us
    unnamed x1, local copies, waits for them, and re-layouts  1.47 us

profile of v4, /device:TPU:0, one launch (start us, length us, event | category | flops | bytes accessed | tf_op | source)
XLA Modules:
  0.0 20.4 jit_solution(13694459861307266086)
XLA Ops:
  0.0 19.0 %shard_map.82 = f32[16,1024]{1,0:T(8,128)} custom-call(f32[3,1024]{1,0:T(4,128)} %points_in.1, f32[16,1024]{1,0:T(8,128)} %charges_in.1, s32[1,1024]{1,0:T(1,128)} %bitcast.1, s32[4,8]{1,0:T(4,128)} %neighbours_in.1, s32[4]{0:T(128)} %counts_in.1, f32[3,1024]{1,0:T(4,128)} %skel_leaf_in.1, f32[3,256]{1,0:T(4,128)} %skel_block_in.1, f32[3,1024]{1,0:T(4,128)} %skel_group_in.1), custom_call_target="tpu_custom_call" | custom-call | tf_op jit(solution)/shard_map/pallas_call | solution.py:384
  19.0 1.5 %copy.10 = f32[16,1024]{1,0:T(8,128)} copy(f32[16,1024]{1,0:T(8,128)} %shard_map.82) | data formatting | bytes 131072

commit v5 on v4

--- a/solution.py
+++ b/solution.py
@@ -61,11 +61,10 @@
         k_lo[at] = (k - hi.astype(f32)).astype(bf16)
 
 
-def times_kernel(v2, k_hi, k_lo, contract=0):
+def times_kernel(v2, k_hi, k_lo):
     half = v2.shape[0] // 2
-    dims = (((1,), (contract,)), ((), ()))
-    r = lax.dot_general(v2, k_hi, dims, preferred_element_type=f32)
-    q = lax.dot_general(v2[:half], k_lo, dims, preferred_element_type=f32)
+    r = jnp.dot(v2, k_hi, preferred_element_type=f32)
+    q = jnp.dot(v2[:half], k_lo, preferred_element_type=f32)
     return r[:half] + r[half:] + q
 
 
@@ -91,10 +90,11 @@
     out,
     points, charges, morton, neighbours, counts, skel_leaf, skel_block, skel_group,
     pad_pts, pad_leaf, pad_grp, pad_blk, pad_left, pad_right, sorted_pts, chg_out, chg_left, chg_right,
-    pts_out, pts_left, pts_right, skel_all, up_out, up_in, bw_all, gw_out, gw_all,
+    pts_out, pts_left, pts_right, up_out, up_in, bw_all, gw_out, gw_all,
     ext_src, ext_c, own_tgt, leaf_src, leaf_tgt, grp_src, grp_tgt, blk_tgt,
     kp_hi, kp_lo, kl_hi, kl_lo, kr_hi, kr_lo, kb_hi, kb_lo, kg_hi, kg_lo, kn_hi, kn_lo,
-    in_sem, halo_send, halo_recv, skel_send, skel_recv, up_send, up_recv, bw_send, bw_recv, gw_send, gw_recv,
+    kd_hi, kd_lo, kc_hi, kc_lo, kt_hi, kt_lo,
+    in_sem, halo_send, halo_recv, up_send, up_recv, bw_send, bw_recv, gw_send, gw_recv,
 ):
     vectors, block_pts = charges.shape
     g = lax.axis_index("grp")
@@ -141,9 +141,8 @@
         return features(pad[...])
 
     loads[0].wait()
-    skel_all[pl.ds(m, 1), 0:3] = skel_block[...][None]
-    skel_all[pl.ds(m, 1), 3:4] = jnp.zeros((1, 1, rank), f32)
-    src_b, tgt = doubled(pad_blk.at[0], skel_block[...])
+    src_b, tgt = doubled(pad_blk, skel_block[...])
+    bw_all[pl.ds(m, 1), vectors:] = pad_blk[...][None]
     blk_tgt[...] = tgt.astype(bf16)
     loads[1].wait()
     src, tgt = doubled(pad_leaf, skel_leaf[...])
@@ -181,9 +180,6 @@
         return pltpu.make_async_remote_copy(
             src_ref=src, dst_ref=dst, send_sem=send, recv_sem=recv, device_id=who, device_id_type=MESH)
 
-    def skel_copy(k, who, slot):
-        return to_peer(skel_all.at[slot], skel_all.at[slot], skel_send.at[k], skel_recv.at[slot], who)
-
     to_right = [
         to_peer(pts_out, pts_left, halo_send.at[0], halo_recv.at[0], right_id),
         to_peer(chg_out, chg_left, halo_send.at[1], halo_recv.at[1], right_id),
@@ -195,9 +191,6 @@
     has_left, has_right = block > 0, block < total - 1
 
     pl.semaphore_wait(barrier, len(greeted))
-    skel_copies = [skel_copy(k, who, m) for k, who in enumerate(peers)]
-    for c in skel_copies:
-        c.start()
 
     @pl.when(has_right)
     def _():
@@ -218,7 +211,7 @@
         leaf_w.append(times_kernel(split_rows(chg_out[:, leaf_cols(i)]), kp_hi[leaf_cols(i)], kp_lo[leaf_cols(i)]))
     lw = jnp.concatenate(leaf_w, axis=1) * scale(leaf_size)
     bw = times_kernel(split_rows(lw), kl_hi[...], kl_lo[...]) * scale(leaf_count * rank)
-    bw_all[pl.ds(m, 1)] = bw[None]
+    bw_all[pl.ds(m, 1), 0:vectors] = bw[None]
     up = times_kernel(split_rows(bw), kr_hi[...], kr_lo[...]) * scale(n_blocks * rank)
     up_out[0] = up[:half]
     up_out[1] = up[half:]
@@ -257,21 +250,15 @@
 
     near = []
     for i in range(leaf_count):
-        rows = (i + 1) * leaf_size
         fill_kernel(
-            ext_src[block_pts : block_pts + rows], own_tgt[:, leaf_cols(i)], kn_hi.at[i], kn_lo.at[i], 0, 0)
-    for i in range(leaf_count):
-        rows = (i + 1) * leaf_size
-        v2 = joined([values(i, leaf_count + j) for j in range(i + 1)])
-        acc = times_kernel(v2, kn_hi[i, 0:rows], kn_lo[i, 0:rows])
-        for j in range(i + 1, leaf_count):
-            acc = acc + times_kernel(
-                split_rows(values(i, leaf_count + j)), kn_hi[j, leaf_cols(i)], kn_lo[j, leaf_cols(i)], 1)
-        near.append(acc)
-
+            ext_src[block_pts : 2 * block_pts], own_tgt[:, leaf_cols(i)], kn_hi.at[i], kn_lo.at[i], 0, 0)
+        v2 = joined([values(i, leaf_count + j) for j in range(leaf_count)])
+        near.append(times_kernel(v2, kn_hi[i, 0:block_pts], kn_lo[i, 0:block_pts]))
+
+    for j, c in enumerate(peers):
+        up_copy(j, c, c[1]).wait_recv()
     gw = up_out[pl.ds(core, 1)][0]
     for j, c in enumerate(peers):
-        up_copy(j, c, c[1]).wait_recv()
         gw = gw + up_in[pl.ds(c[1], 1)][0]
     gw_out[...] = gw
     gw_copies = [gw_copy(k, who, g, core) for k, who in enumerate(cousins)]
@@ -292,17 +279,20 @@
         fill_kernel(grp_src[cousin_rows(d)], grp_tgt[...], kg_hi.at[d - 1], kg_lo.at[d - 1], 0, 0)
 
     def fill_peer(d):
-        src, _ = doubled(pad_blk.at[d], skel_all[lax.rem(m + d, n_blocks)][0:3])
+        src, _ = features(bw_all[lax.rem(m + d, n_blocks)][vectors:])
         fill_kernel(src.T.astype(bf16), blk_tgt[...], kb_hi.at[d - 1], kb_lo.at[d - 1], 0, 0)
 
     def add_peer(d, acc):
-        v2 = split_rows(bw_all[lax.rem(m + d, n_blocks)])
+        v2 = split_rows(bw_all[lax.rem(m + d, n_blocks)][:vectors])
         return acc + times_kernel(v2, kb_hi[d - 1], kb_lo[d - 1])
 
     repeat(n_groups, fill_group)
-    for j, c in enumerate(peers):
-        skel_copy(j, c, c[1]).wait_recv()
-    repeat(n_blocks, fill_peer)
+    blk_src = src_b.T.astype(bf16)
+    own_rows = pl.ds(pl.multiple_of(g * rank, rank), rank)
+    fill_kernel(grp_src[own_rows], blk_tgt[...], kd_hi, kd_lo, 0, 0)
+    for i in range(leaf_count):
+        fill_kernel(blk_src, leaf_tgt[:, rank_cols(i)], kc_hi, kc_lo, 0, i * rank)
+        fill_kernel(leaf_src[rank_cols(i)], own_tgt[:, leaf_cols(i)], kt_hi, kt_lo, i * rank, 0)
 
     def halo(there, copies, pts, chg, pad, base):
         @pl.when(there)
@@ -337,6 +327,7 @@
     bw_copy(0, twin, twin).wait_recv()
     for c in same_core:
         bw_copy(0, twin, lax.rem(c + twin - m + n_blocks, n_blocks)).wait_recv()
+    repeat(n_blocks, fill_peer)
     field = gather_terms(n_blocks, add_peer, empty) * scale((n_blocks - 1) * rank)
     for d in range(1, n_groups):
         for part in range(2):
@@ -348,10 +339,10 @@
         return acc + times_kernel(v2, kg_hi[d - 1], kg_lo[d - 1])
 
     gfield = gather_terms(n_groups, add_group, empty) * scale((n_groups - 1) * rank)
-    field = field + scale(rank) * times_kernel(split_rows(gfield), kr_hi[...], kr_lo[...], 1)
-    lf = times_kernel(split_rows(field), kl_hi[...], kl_lo[...], 1) * scale(rank)
-    for i in range(leaf_count):
-        far = times_kernel(split_rows(lf[:, rank_cols(i)]), kp_hi[leaf_cols(i)], kp_lo[leaf_cols(i)], 1)
+    field = field + scale(rank) * times_kernel(split_rows(gfield), kd_hi[...], kd_lo[...])
+    lf = times_kernel(split_rows(field), kc_hi[...], kc_lo[...]) * scale(rank)
+    for i in range(leaf_count):
+        far = times_kernel(split_rows(lf[:, rank_cols(i)]), kt_hi[rank_cols(i)], kt_lo[rank_cols(i)])
         out[:, leaf_cols(i)] = near[i] * scale(leaf_size) + far * scale(rank)
 
     @pl.when(has_right)
@@ -364,7 +355,7 @@
         for c in to_left:
             c.wait_send()
 
-    for c in skel_copies + up_copies + bw_copies + forwards + gw_copies:
+    for c in up_copies + bw_copies + forwards + gw_copies:
         c.wait_send()
 
 
@@ -391,7 +382,7 @@
             pltpu.VMEM((ROWS, block_pts), f32),
             pltpu.VMEM((ROWS, leaf_cols), f32),
             pltpu.VMEM((ROWS, n_groups * rank), f32),
-            pltpu.VMEM((n_blocks, ROWS, rank), f32),
+            pltpu.VMEM((ROWS, rank), f32),
             pltpu.VMEM((ROWS, block_pts), f32),
             pltpu.VMEM((ROWS, block_pts), f32),
             pltpu.VMEM((ROWS, block_pts), f32),
@@ -401,10 +392,9 @@
             pltpu.VMEM((SENT, block_pts), f32),
             pltpu.VMEM((SENT, block_pts), f32),
             pltpu.VMEM((SENT, block_pts), f32),
-            pltpu.VMEM((n_blocks, SENT, rank), f32),
             pltpu.VMEM((2, vectors // 2, rank), f32),
             pltpu.VMEM((n_blocks, vectors // 2, rank), f32),
-            pltpu.VMEM((n_blocks, vectors, rank), f32),
+            pltpu.VMEM((n_blocks, vectors + ROWS, rank), f32),
             pltpu.VMEM((vectors // 2, rank), f32),
             pltpu.VMEM((n_groups, 2, vectors // 2, rank), f32),
             pltpu.VMEM((3 * block_pts, FEAT), bf16),
@@ -421,11 +411,12 @@
             *both(n_blocks - 1, rank, rank),
             *both(n_groups - 1, rank, rank),
             *both(leaf_count, window, leaf_size),
+            *both(rank, rank),
+            *both(rank, leaf_cols),
+            *both(leaf_cols, leaf_size),
             dma((len(operands),)),
             dma((4,)),
             dma((4,)),
-            dma((n_blocks - 1,)),
-            dma((n_blocks,)),
             dma((n_blocks - 1,)),
             dma((n_blocks,)),
             dma((n_blocks,)),

time: 20.6 us -> 20.5 us (level)
  no operation moved by 1% of the time
where the time goes in v5:
time: 20.5 us; the launch traced here: 20.3 us
  Pallas kernels  18.8 us (92%)
  local copies, waits for them, and re-layouts  1.47 us (7%)
    pallas_call x1, Pallas kernels, body(): pl.pallas_call(functools.partial(kernel, n_groups, n_blocks, leaf_count,...  18.8 us
    unnamed x1, local copies, waits for them, and re-layouts  1.47 us

profile of v5, /device:TPU:0, one launch (start us, length us, event | category | flops | bytes accessed | tf_op | source)
XLA Modules:
  0.0 20.3 jit_solution(4426641361404117748)
XLA Ops:
  0.0 18.8 %shard_map.82 = f32[16,1024]{1,0:T(8,128)} custom-call(f32[3,1024]{1,0:T(4,128)} %points_in.1, f32[16,1024]{1,0:T(8,128)} %charges_in.1, s32[1,1024]{1,0:T(1,128)} %bitcast.1, s32[4,8]{1,0:T(4,128)} %neighbours_in.1, s32[4]{0:T(128)} %counts_in.1, f32[3,1024]{1,0:T(4,128)} %skel_leaf_in.1, f32[3,256]{1,0:T(4,128)} %skel_block_in.1, f32[3,1024]{1,0:T(4,128)} %skel_group_in.1), custom_call_target="tpu_custom_call" | custom-call | tf_op jit(solution)/shard_map/pallas_call | solution.py:375
  18.8 1.5 %copy.10 = f32[16,1024]{1,0:T(8,128)} copy(f32[16,1024]{1,0:T(8,128)} %shard_map.82) | data formatting | bytes 131072

commit v6 on v5

--- a/solution.py
+++ b/solution.py
@@ -89,7 +89,7 @@
     points_in, charges_in, morton_in, neighbours_in, counts_in, skel_leaf_in, skel_block_in, skel_group_in,
     out,
     points, charges, morton, neighbours, counts, skel_leaf, skel_block, skel_group,
-    pad_pts, pad_leaf, pad_grp, pad_blk, pad_left, pad_right, sorted_pts, chg_out, chg_left, chg_right,
+    pad_pts, pad_leaf, pad_grp, pad_own, pad_blk, pad_left, pad_right, sorted_pts, chg_out, chg_left, chg_right,
     pts_out, pts_left, pts_right, up_out, up_in, bw_all, gw_out, gw_all,
     ext_src, ext_c, own_tgt, leaf_src, leaf_tgt, grp_src, grp_tgt, blk_tgt,
     kp_hi, kp_lo, kl_hi, kl_lo, kr_hi, kr_lo, kb_hi, kb_lo, kg_hi, kg_lo, kn_hi, kn_lo,
@@ -140,24 +140,7 @@
         pad[3:6] = coords
         return features(pad[...])
 
-    loads[0].wait()
-    src_b, tgt = doubled(pad_blk, skel_block[...])
-    bw_all[pl.ds(m, 1), vectors:] = pad_blk[...][None]
-    blk_tgt[...] = tgt.astype(bf16)
-    loads[1].wait()
-    src, tgt = doubled(pad_leaf, skel_leaf[...])
-    leaf_src[...] = src.T.astype(bf16)
-    leaf_tgt[...] = tgt.astype(bf16)
-    fill_kernel(leaf_src[...], blk_tgt[...], kl_hi, kl_lo, 0, 0)
-    loads[2].wait()
-    src, tgt = doubled(pad_grp, skel_group[...])
-    grp_src[...] = src.T.astype(bf16)
-    for j in range(n_groups):
-        pl.when(g == j)(functools.partial(
-            grp_tgt.__setitem__, (slice(None), slice(None)), tgt[:, rank_cols(j)].astype(bf16)))
-    fill_kernel(src_b.T.astype(bf16), grp_tgt[...], kr_hi, kr_lo, 0, 0)
-
-    for c in loads[3:6]:
+    for c in loads:
         c.wait()
     pad_pts[6:8] = jnp.zeros((2, block_pts), f32)
     pad_pts[0:3] = points[...]
@@ -176,6 +159,33 @@
         chg_out[:, leaf_cols(i)] = s[32 : 32 + vectors] + s[32 + vectors :]
     pts_out[...] = sorted_pts[0:SENT]
 
+    own_rows = pl.ds(pl.multiple_of(g * rank, rank), rank)
+    src_b, tgt = doubled(pad_blk, skel_block[...])
+    bw_all[pl.ds(m, 1), vectors:] = pad_blk[...][None]
+    blk_tgt[...] = tgt.astype(bf16)
+    blk_src = src_b.T.astype(bf16)
+    src, tgt = doubled(pad_leaf, skel_leaf[...])
+    leaf_src[...] = src.T.astype(bf16)
+    leaf_tgt[...] = tgt.astype(bf16)
+    _, tgt = doubled(pad_own, skel_group[:, own_rows])
+    grp_tgt[...] = tgt.astype(bf16)
+    fill_kernel(leaf_src[...], blk_tgt[...], kl_hi, kl_lo, 0, 0)
+    fill_kernel(blk_src, grp_tgt[...], kr_hi, kr_lo, 0, 0)
+
+    src, tgt = features(sorted_pts[...])
+    ext_src[block_pts : 2 * block_pts] = src.T.astype(bf16)
+    own_tgt[...] = tgt.astype(bf16)
+    leaf_w = []
+    for i in range(leaf_count):
+        fill_kernel(ext_src[leaf_cols(leaf_count + i)], leaf_tgt[:, rank_cols(i)], kp_hi, kp_lo, i * leaf_size, 0)
+        leaf_w.append(times_kernel(split_rows(chg_out[:, leaf_cols(i)]), kp_hi[leaf_cols(i)], kp_lo[leaf_cols(i)]))
+    lw = jnp.concatenate(leaf_w, axis=1) * scale(leaf_size)
+    bw = times_kernel(split_rows(lw), kl_hi[...], kl_lo[...]) * scale(leaf_count * rank)
+    bw_all[pl.ds(m, 1), 0:vectors] = bw[None]
+    up = times_kernel(split_rows(bw), kr_hi[...], kr_lo[...]) * scale(n_blocks * rank)
+    up_out[0] = up[:half]
+    up_out[1] = up[half:]
+
     def to_peer(src, dst, send, recv, who):
         return pltpu.make_async_remote_copy(
             src_ref=src, dst_ref=dst, send_sem=send, recv_sem=recv, device_id=who, device_id_type=MESH)
@@ -190,7 +200,20 @@
     ]
     has_left, has_right = block > 0, block < total - 1
 
+    def up_copy(k, who, slot):
+        return to_peer(up_out.at[lax.rem(who[1], 2)], up_in.at[slot], up_send.at[k], up_recv.at[slot], who)
+
+    def bw_copy(k, who, slot):
+        return to_peer(bw_all.at[slot], bw_all.at[slot], bw_send.at[k], bw_recv.at[slot], (g, who))
+
+    def gw_copy(k, who, group, part):
+        return to_peer(gw_out, gw_all.at[group, part], gw_send.at[k], gw_recv.at[group, part], who)
+
+    up_copies = [up_copy(k, who, m) for k, who in enumerate(peers)]
+    bw_copies = [bw_copy(k, who, m) for k, who in enumerate([twin] + same_core)]
     pl.semaphore_wait(barrier, len(greeted))
+    for c in up_copies + bw_copies:
+        c.start()
 
     @pl.when(has_right)
     def _():
@@ -202,37 +225,7 @@
         for c in to_left:
             c.start()
 
-    src, tgt = features(sorted_pts[...])
-    ext_src[block_pts : 2 * block_pts] = src.T.astype(bf16)
-    own_tgt[...] = tgt.astype(bf16)
-    leaf_w = []
-    for i in range(leaf_count):
-        fill_kernel(ext_src[leaf_cols(leaf_count + i)], leaf_tgt[:, rank_cols(i)], kp_hi, kp_lo, i * leaf_size, 0)
-        leaf_w.append(times_kernel(split_rows(chg_out[:, leaf_cols(i)]), kp_hi[leaf_cols(i)], kp_lo[leaf_cols(i)]))
-    lw = jnp.concatenate(leaf_w, axis=1) * scale(leaf_size)
-    bw = times_kernel(split_rows(lw), kl_hi[...], kl_lo[...]) * scale(leaf_count * rank)
-    bw_all[pl.ds(m, 1), 0:vectors] = bw[None]
-    up = times_kernel(split_rows(bw), kr_hi[...], kr_lo[...]) * scale(n_blocks * rank)
-    up_out[0] = up[:half]
-    up_out[1] = up[half:]
-
-    def up_copy(k, who, slot):
-        return to_peer(up_out.at[lax.rem(who[1], 2)], up_in.at[slot], up_send.at[k], up_recv.at[slot], who)
-
-    def bw_copy(k, who, slot):
-        return to_peer(bw_all.at[slot], bw_all.at[slot], bw_send.at[k], bw_recv.at[slot], (g, who))
-
-    def gw_copy(k, who, group, part):
-        return to_peer(gw_out, gw_all.at[group, part], gw_send.at[k], gw_recv.at[group, part], who)
-
-    up_copies = [up_copy(k, who, m) for k, who in enumerate(peers)]
-    bw_copies = [bw_copy(k, who, m) for k, who in enumerate([twin] + same_core)]
-    for c in up_copies + bw_copies:
-        c.start()
-
     ext_c[:, block_pts : 2 * block_pts] = chg_out[...]
-    loads[6].wait()
-    loads[7].wait()
     first_leaf = block * leaf_count - leaf_count
 
     def values(i, e):
@@ -255,8 +248,24 @@
         v2 = joined([values(i, leaf_count + j) for j in range(leaf_count)])
         near.append(times_kernel(v2, kn_hi[i, 0:block_pts], kn_lo[i, 0:block_pts]))
 
+    src, _ = doubled(pad_grp, skel_group[...])
+    grp_src[...] = src.T.astype(bf16)
+
+    def cousin_rows(d):
+        return pl.ds(pl.multiple_of(lax.rem(g + d, n_groups) * rank, rank), rank)
+
+    def fill_group(d):
+        fill_kernel(grp_src[cousin_rows(d)], grp_tgt[...], kg_hi.at[d - 1], kg_lo.at[d - 1], 0, 0)
+
+    repeat(n_groups, fill_group)
+    fill_kernel(grp_src[own_rows], blk_tgt[...], kd_hi, kd_lo, 0, 0)
+    for i in range(leaf_count):
+        fill_kernel(blk_src, leaf_tgt[:, rank_cols(i)], kc_hi, kc_lo, 0, i * rank)
+        fill_kernel(leaf_src[rank_cols(i)], own_tgt[:, leaf_cols(i)], kt_hi, kt_lo, i * rank, 0)
+
     for j, c in enumerate(peers):
         up_copy(j, c, c[1]).wait_recv()
+
     gw = up_out[pl.ds(core, 1)][0]
     for j, c in enumerate(peers):
         gw = gw + up_in[pl.ds(c[1], 1)][0]
@@ -272,12 +281,6 @@
 
     empty = jnp.zeros((vectors, rank), f32)
 
-    def cousin_rows(d):
-        return pl.ds(pl.multiple_of(lax.rem(g + d, n_groups) * rank, rank), rank)
-
-    def fill_group(d):
-        fill_kernel(grp_src[cousin_rows(d)], grp_tgt[...], kg_hi.at[d - 1], kg_lo.at[d - 1], 0, 0)
-
     def fill_peer(d):
         src, _ = features(bw_all[lax.rem(m + d, n_blocks)][vectors:])
         fill_kernel(src.T.astype(bf16), blk_tgt[...], kb_hi.at[d - 1], kb_lo.at[d - 1], 0, 0)
@@ -286,13 +289,6 @@
         v2 = split_rows(bw_all[lax.rem(m + d, n_blocks)][:vectors])
         return acc + times_kernel(v2, kb_hi[d - 1], kb_lo[d - 1])
 
-    repeat(n_groups, fill_group)
-    blk_src = src_b.T.astype(bf16)
-    own_rows = pl.ds(pl.multiple_of(g * rank, rank), rank)
-    fill_kernel(grp_src[own_rows], blk_tgt[...], kd_hi, kd_lo, 0, 0)
-    for i in range(leaf_count):
-        fill_kernel(blk_src, leaf_tgt[:, rank_cols(i)], kc_hi, kc_lo, 0, i * rank)
-        fill_kernel(leaf_src[rank_cols(i)], own_tgt[:, leaf_cols(i)], kt_hi, kt_lo, i * rank, 0)
 
     def halo(there, copies, pts, chg, pad, base):
         @pl.when(there)
@@ -329,6 +325,19 @@
         bw_copy(0, twin, lax.rem(c + twin - m + n_blocks, n_blocks)).wait_recv()
     repeat(n_blocks, fill_peer)
     field = gather_terms(n_blocks, add_peer, empty) * scale((n_blocks - 1) * rank)
+    @pl.when(has_right)
+    def _():
+        for c in to_right:
+            c.wait_send()
+
+    @pl.when(has_left)
+    def _():
+        for c in to_left:
+            c.wait_send()
+
+    for c in up_copies + bw_copies + forwards + gw_copies:
+        c.wait_send()
+
     for d in range(1, n_groups):
         for part in range(2):
             gw_copy(0, cousins[0], lax.rem(g + d, n_groups), part).wait_recv()
@@ -344,19 +353,6 @@
     for i in range(leaf_count):
         far = times_kernel(split_rows(lf[:, rank_cols(i)]), kt_hi[rank_cols(i)], kt_lo[rank_cols(i)])
         out[:, leaf_cols(i)] = near[i] * scale(leaf_size) + far * scale(rank)
-
-    @pl.when(has_right)
-    def _():
-        for c in to_right:
-            c.wait_send()
-
-    @pl.when(has_left)
-    def _():
-        for c in to_left:
-            c.wait_send()
-
-    for c in up_copies + bw_copies + forwards + gw_copies:
-        c.wait_send()
 
 
 def body(n_groups, n_blocks, points, charges, morton, neighbours, counts, skel_leaf, skel_block, skel_group):
@@ -382,6 +378,7 @@
             pltpu.VMEM((ROWS, block_pts), f32),
             pltpu.VMEM((ROWS, leaf_cols), f32),
             pltpu.VMEM((ROWS, n_groups * rank), f32),
+            pltpu.VMEM((ROWS, rank), f32),
             pltpu.VMEM((ROWS, rank), f32),
             pltpu.VMEM((ROWS, block_pts), f32),
             pltpu.VMEM((ROWS, block_pts), f32),

time: 20.5 us -> 18.2 us (0.89)
  the two profiles are of different devices: /device:TPU:0 before, /device:TPU:4 now
where the time goes in v6:
time: 18.2 us; the launch traced here: 18 us
  Pallas kernels  16.5 us (91%)
  local copies, waits for them, and re-layouts  1.47 us (8%)
    pallas_call x1, Pallas kernels, body(): pl.pallas_call(functools.partial(kernel, n_groups, n_blocks, leaf_count,...  16.5 us
    unnamed x1, local copies, waits for them, and re-layouts  1.47 us

profile of v6, /device:TPU:4, one launch (start us, length us, event | category | flops | bytes accessed | tf_op | source)
XLA Modules:
  0.0 18.0 jit_solution(12725824294080337435)
XLA Ops:
  0.0 16.5 %shard_map.82 = f32[16,1024]{1,0:T(8,128)} custom-call(f32[3,1024]{1,0:T(4,128)} %points_in.1, f32[16,1024]{1,0:T(8,128)} %charges_in.1, s32[1,1024]{1,0:T(1,128)} %bitcast.1, s32[4,8]{1,0:T(4,128)} %neighbours_in.1, s32[4]{0:T(128)} %counts_in.1, f32[3,1024]{1,0:T(4,128)} %skel_leaf_in.1, f32[3,256]{1,0:T(4,128)} %skel_block_in.1, f32[3,1024]{1,0:T(4,128)} %skel_group_in.1), custom_call_target="tpu_custom_call" | custom-call | tf_op jit(solution)/shard_map/pallas_call | solution.py:371
  16.6 1.5 %copy.10 = f32[16,1024]{1,0:T(8,128)} copy(f32[16,1024]{1,0:T(8,128)} %shard_map.82) | data formatting | bytes 131072

commit v7 on v6

--- a/solution.py
+++ b/solution.py
@@ -212,7 +212,7 @@
     up_copies = [up_copy(k, who, m) for k, who in enumerate(peers)]
     bw_copies = [bw_copy(k, who, m) for k, who in enumerate([twin] + same_core)]
     pl.semaphore_wait(barrier, len(greeted))
-    for c in up_copies + bw_copies:
+    for c in up_copies:
         c.start()
 
     @pl.when(has_right)
@@ -224,6 +224,9 @@
     def _():
         for c in to_left:
             c.start()
+
+    for c in bw_copies:
+        c.start()
 
     ext_c[:, block_pts : 2 * block_pts] = chg_out[...]
     first_leaf = block * leaf_count - leaf_count
@@ -273,11 +276,6 @@
     gw_copies = [gw_copy(k, who, g, core) for k, who in enumerate(cousins)]
     for c in gw_copies:
         c.start()
-    forwards = []
-    for k, c in enumerate(same_core):
-        bw_copy(0, twin, c).wait_recv()
-        forwards.append(bw_copy(1 + len(same_core) + k, twin, c))
-        forwards[-1].start()
 
     empty = jnp.zeros((vectors, rank), f32)
 
@@ -320,10 +318,17 @@
         v2 = joined([values(i, e) for e in before + after])
         near[i] = near[i] + times_kernel(v2, kn_hi[i, base:end], kn_lo[i, base:end])
 
+    forwards = []
+    for k, c in enumerate(same_core):
+        bw_copy(0, twin, c).wait_recv()
+        forwards.append(bw_copy(1 + len(same_core) + k, twin, c))
+        forwards[-1].start()
+
+    repeat(n_blocks // 2, lambda k: fill_peer(2 * k))
     bw_copy(0, twin, twin).wait_recv()
     for c in same_core:
         bw_copy(0, twin, lax.rem(c + twin - m + n_blocks, n_blocks)).wait_recv()
-    repeat(n_blocks, fill_peer)
+    repeat(n_blocks // 2 + 1, lambda k: fill_peer(2 * k - 1))
     field = gather_terms(n_blocks, add_peer, empty) * scale((n_blocks - 1) * rank)
     @pl.when(has_right)
     def _():

time: 18.2 us -> 18.1 us (level)
  the two profiles are of different devices: /device:TPU:4 before, /device:TPU:5 now
where the time goes in v7:
time: 18.1 us; the launch traced here: 17.9 us
  Pallas kernels  16.4 us (91%)
  local copies, waits for them, and re-layouts  1.47 us (8%)
    pallas_call x1, Pallas kernels, body(): pl.pallas_call(functools.partial(kernel, n_groups, n_blocks, leaf_count,...  16.4 us
    unnamed x1, local copies, waits for them, and re-layouts  1.47 us

profile of v7, /device:TPU:5, one launch (start us, length us, event | category | flops | bytes accessed | tf_op | source)
XLA Modules:
  0.0 17.9 jit_solution(5671321366467846255)
XLA Ops:
  0.0 16.4 %shard_map.82 = f32[16,1024]{1,0:T(8,128)} custom-call(f32[3,1024]{1,0:T(4,128)} %points_in.1, f32[16,1024]{1,0:T(8,128)} %charges_in.1, s32[1,1024]{1,0:T(1,128)} %bitcast.1, s32[4,8]{1,0:T(4,128)} %neighbours_in.1, s32[4]{0:T(128)} %counts_in.1, f32[3,1024]{1,0:T(4,128)} %skel_leaf_in.1, f32[3,256]{1,0:T(4,128)} %skel_block_in.1, f32[3,1024]{1,0:T(4,128)} %skel_group_in.1), custom_call_target="tpu_custom_call" | custom-call | tf_op jit(solution)/shard_map/pallas_call | solution.py:376
  16.4 1.5 %copy.10 = f32[16,1024]{1,0:T(8,128)} copy(f32[16,1024]{1,0:T(8,128)} %shard_map.82) | data formatting | bytes 131072

commit v8 on v7

--- a/solution.py
+++ b/solution.py
@@ -159,6 +159,32 @@
         chg_out[:, leaf_cols(i)] = s[32 : 32 + vectors] + s[32 + vectors :]
     pts_out[...] = sorted_pts[0:SENT]
 
+    def to_peer(src, dst, send, recv, who):
+        return pltpu.make_async_remote_copy(
+            src_ref=src, dst_ref=dst, send_sem=send, recv_sem=recv, device_id=who, device_id_type=MESH)
+
+    to_right = [
+        to_peer(pts_out, pts_left, halo_send.at[0], halo_recv.at[0], right_id),
+        to_peer(chg_out, chg_left, halo_send.at[1], halo_recv.at[1], right_id),
+    ]
+    to_left = [
+        to_peer(pts_out, pts_right, halo_send.at[2], halo_recv.at[2], left_id),
+        to_peer(chg_out, chg_right, halo_send.at[3], halo_recv.at[3], left_id),
+    ]
+    has_left, has_right = block > 0, block < total - 1
+
+    pl.semaphore_wait(barrier, len(greeted))
+
+    @pl.when(has_right)
+    def _():
+        for c in to_right:
+            c.start()
+
+    @pl.when(has_left)
+    def _():
+        for c in to_left:
+            c.start()
+
     own_rows = pl.ds(pl.multiple_of(g * rank, rank), rank)
     src_b, tgt = doubled(pad_blk, skel_block[...])
     bw_all[pl.ds(m, 1), vectors:] = pad_blk[...][None]
@@ -186,20 +212,6 @@
     up_out[0] = up[:half]
     up_out[1] = up[half:]
 
-    def to_peer(src, dst, send, recv, who):
-        return pltpu.make_async_remote_copy(
-            src_ref=src, dst_ref=dst, send_sem=send, recv_sem=recv, device_id=who, device_id_type=MESH)
-
-    to_right = [
-        to_peer(pts_out, pts_left, halo_send.at[0], halo_recv.at[0], right_id),
-        to_peer(chg_out, chg_left, halo_send.at[1], halo_recv.at[1], right_id),
-    ]
-    to_left = [
-        to_peer(pts_out, pts_right, halo_send.at[2], halo_recv.at[2], left_id),
-        to_peer(chg_out, chg_right, halo_send.at[3], halo_recv.at[3], left_id),
-    ]
-    has_left, has_right = block > 0, block < total - 1
-
     def up_copy(k, who, slot):
         return to_peer(up_out.at[lax.rem(who[1], 2)], up_in.at[slot], up_send.at[k], up_recv.at[slot], who)
 
@@ -211,19 +223,8 @@
 
     up_copies = [up_copy(k, who, m) for k, who in enumerate(peers)]
     bw_copies = [bw_copy(k, who, m) for k, who in enumerate([twin] + same_core)]
-    pl.semaphore_wait(barrier, len(greeted))
     for c in up_copies:
         c.start()
-
-    @pl.when(has_right)
-    def _():
-        for c in to_right:
-            c.start()
-
-    @pl.when(has_left)
-    def _():
-        for c in to_left:
-            c.start()
 
     for c in bw_copies:
         c.start()

time: 18.1 us -> 18.7 us (1.033)
  the two profiles are of different devices: /device:TPU:5 before, /device:TPU:0 now
where the time goes in v8:
time: 18.7 us; the launch traced here: 18.5 us
  Pallas kernels  17 us (91%)
  local copies, waits for them, and re-layouts  1.47 us (8%)
    pallas_call x1, Pallas kernels, body(): pl.pallas_call(functools.partial(kernel, n_groups, n_blocks, leaf_count,...  17 us
    unnamed x1, local copies, waits for them, and re-layouts  1.47 us

profile of v8, /device:TPU:0, one launch (start us, length us, event | category | flops | bytes accessed | tf_op | source)
XLA Modules:
  0.0 18.5 jit_solution(18312186512336520131)
XLA Ops:
  0.0 17.0 %shard_map.82 = f32[16,1024]{1,0:T(8,128)} custom-call(f32[3,1024]{1,0:T(4,128)} %points_in.1, f32[16,1024]{1,0:T(8,128)} %charges_in.1, s32[1,1024]{1,0:T(1,128)} %bitcast.1, s32[4,8]{1,0:T(4,128)} %neighbours_in.1, s32[4]{0:T(128)} %counts_in.1, f32[3,1024]{1,0:T(4,128)} %skel_leaf_in.1, f32[3,256]{1,0:T(4,128)} %skel_block_in.1, f32[3,1024]{1,0:T(4,128)} %skel_group_in.1), custom_call_target="tpu_custom_call" | custom-call | tf_op jit(solution)/shard_map/pallas_call | solution.py:377
  17.0 1.5 %copy.10 = f32[16,1024]{1,0:T(8,128)} copy(f32[16,1024]{1,0:T(8,128)} %shard_map.82) | data formatting | bytes 131072
